TPU v7x, 32 devices: a whole 2x2x4 slice. The times are simulated.
32 devices in a mesh: dom: 16 (over z, y, x), off: 2 (over core).
Axes of the slice: x: 2, y: 2, z: 4, core: 2. Of those that a mesh axis runs over, the one named last changes fastest.
Arguments:
- contrib: float32 [384, 2432], P('dom'), may hold values from -6 to 6
- slot_octant: int32 [384], P('dom'), may hold values from 0 to 255, as said below
- vlist_src: int32 [256, 40], P('dom'), may hold values from 0 to 255, as said below
- vlist_class: int32 [256, 40], P('dom'), may hold values from 0 to 79, as said below
- translation: float32 [80, 152, 152], P('off'), may hold values from -0.078125 to 0.078125
Outputs:
- potential: float32 [256, 2432], P(('dom', 'off'))
Inputs may be any that keep to these rules, and one draw needn't show every extreme that they name: `slot_octant`: slot k < 16 of partition p names octant p * 16 + k; its other slots name octants p * 16 + j with -4 <= j < 20, taken modulo 256, and each partition has one slot at j = -4 and one at j = 19. vlist_src[t, l] = t + d modulo 256, where the nonzero offset d, with |d| <= 12, depends only on the class vlist_class[t, l]; some class has d = 12 and some d = -12. `vlist_class`: the 40 classes of one octant are all different, and every class is used by some octant.
All inputs are finite; a program needn't handle non-finite values.
Results may differ from a plain program's by a relative error of at most 0.00007.
Values sent between devices are 32-bit elements; how exact they have to be, the bound alone decides.
No kernel may reach another device: no remote copies, remote signals or barrier semaphores. Data moves between devices by JAX's collectives and lax.ppermute only.
A program may use at most 64 MiB of HBM per device.

v0:
```python
import jax
import jax.numpy as jnp
from jax import lax
from jax.sharding import PartitionSpec as P

E = 152
R = 16
TGT = 16
SPILL = 4


class_group = 8


def padded(block, sides, width):
    for axis, dim in sides:
        count = lax.axis_size(axis)
        forward = [(i, i + 1) for i in range(count - 1)]
        forward.append((count - 1, 0))
        backward = [(target, source) for source, target in forward]
        low = lax.ppermute(
            lax.slice_in_dim(block, block.shape[dim] - width, None, axis=dim), axis, forward
        )
        high = lax.ppermute(lax.slice_in_dim(block, 0, width, axis=dim), axis, backward)
        block = jnp.concatenate([low, block, high], axis=dim)
    return block


def spread_rows(local_ids, values, count):
    columns = jnp.arange(count)
    onehot = (local_ids[:, None] == columns[None, :]).astype(jnp.float32)
    return jnp.dot(
        onehot.T, values, precision=lax.Precision.HIGHEST, preferred_element_type=jnp.float32
    )


def local(contrib, slot_octant, vlist_src, vlist_class, translation):
    octants = TGT * lax.axis_size("dom")
    reach = TGT - SPILL
    position = lax.axis_index("dom")
    first_octant = position * TGT - SPILL
    local_ids = (slot_octant - first_octant + octants) % octants
    table = spread_rows(local_ids, contrib, TGT + 2 * SPILL)
    widened = padded(table, (("dom", 0),), TGT)
    lower = widened[:TGT]
    middle = widened[TGT : 2 * TGT + 2 * SPILL]
    upper = widened[2 * TGT + 2 * SPILL :]
    window = jnp.pad(lower, ((0, 2 * TGT - 2 * SPILL), (0, 0)))
    window = window + jnp.pad(middle, ((TGT - 2 * SPILL, TGT - 2 * SPILL), (0, 0)))
    window = window + jnp.pad(upper, ((2 * TGT - 2 * SPILL, 0), (0, 0)))
    window_start = position * TGT - reach
    window_ids = (vlist_src - window_start + octants) % octants
    targets = vlist_src.shape[0]
    class_count = translation.shape[0]
    first_class = lax.axis_index("off") * class_count

    def class_block(running, block_index):
        classes = first_class + block_index * class_group + jnp.arange(class_group, dtype=jnp.int32)
        matches = vlist_class[:, :, None] == classes[None, None, :]
        chosen = jnp.max(jnp.where(matches, window_ids[:, :, None], -1), axis=1)
        present = (chosen >= 0).astype(jnp.float32)
        sources = window[jnp.maximum(chosen, 0)] * present[:, :, None]
        sources = sources.reshape(targets, class_group, E, R)
        blocks = lax.dynamic_slice_in_dim(translation, block_index * class_group, class_group, 0)
        running = running + jnp.einsum(
            "cij,tcjr->tir", blocks, sources, precision=lax.Precision.HIGHEST
        )
        return (running, None)

    running, ignored = lax.scan(
        class_block,
        jnp.zeros((targets, E, R), jnp.float32),
        jnp.arange(class_count // class_group, dtype=jnp.int32),
    )
    partial_sum = running.reshape(targets, E * R)
    whole = lax.psum(partial_sum, "off")
    share = targets // lax.axis_size("off")
    return lax.dynamic_slice_in_dim(whole, lax.axis_index("off") * share, share, 0)


def solution(mesh):
    return jax.shard_map(
        local,
        mesh=mesh,
        in_specs=(P("dom", None), P("dom"), P("dom", None), P("dom", None), P("off", None, None)),
        out_specs=P(("dom", "off"), None),
        check_vma=False,
    )
```

profile of v0, /device:TPU:0, one launch (start us, length us, event | category | flops | bytes accessed | tf_op | source)
XLA Modules:
  0.0 186.7 jit_solution(1085379565776952419)
XLA Ops:
  6.5 0.7 and_select_fusion
  7.9 3.0 %collective-permute-start = (f32[16,2432]{1,0:T(8,128)S(1)}, f32[16,2432]{1,0:T(8,128)S(1)}, u32[]{:S(2)}, u32[]{:S(2)}) collective-permute-start(f32[16,2432]{1,0:T(8,128)S(1)} %get-tuple-element.91), channel_id=1, source_target_pairs={{0,2},{2,4},{4,6},{6,8},{8,10},{10,12},{12,14},{14,16},{16,18},{18... | collective-permute-start | bytes 466952 | tf_op jit(solution)/shard_map/ppermute | solution.py:21
  10.9 4.1 %collective-permute-start.1 = (f32[16,2432]{1,0:T(8,128)S(1)}, f32[16,2432]{1,0:T(8,128)S(1)}, u32[]{:S(2)}, u32[]{:S(2)}) collective-permute-start(f32[16,2432]{1,0:T(8,128)S(1)} %get-tuple-element.92), channel_id=1, source_target_pairs={{2,0},{4,2},{6,4},{8,6},{10,8},{12,10},{14,12},{16,14},{18,16},{20... | collective-permute-start | bytes 466952 | tf_op jit(solution)/shard_map/ppermute | solution.py:24
  15.0 0.7 add_select_fusion
  15.7 3.4 %collective-permute-done = f32[16,2432]{1,0:T(8,128)S(1)} collective-permute-done((f32[16,2432]{1,0:T(8,128)S(1)}, f32[16,2432]{1,0:T(8,128)S(1)}, u32[]{:S(2)}, u32[]{:S(2)}) %collective-permute-start) | collective-permute-done | bytes 155680 | tf_op jit(solution)/shard_map/ppermute | solution.py:21
  19.5 138.6 %while.11 = (s32[]{:T(128)}, f32[16,152,16]{1,2,0:T(8,128)S(1)}, s32[16,40]{1,0:T(8,128)}, s32[5]{0:T(128)S(1)}, s32[]{:T(128)}, /*index=5*/s32[16,40]{1,0:T(8,1...) while((s32[]{:T(128)}, f32[16,152,16]{1,2,0:T(8,128)S(1)}, ...), condition=%wide.region_2.3_spmd.clone, body=%wide.region_0.2_spmd.clone.sunk | while | flops 568209664 | bytes 16513293 | solution.py:70
  19.5 0.7 dynamic_slice.25
  20.8 1.1 select_reduce_fusion.2
  22.1 1.1 gather_fusion
  23.1 5.4 %gather.12 = f32[16,8,152,16]{3,2,1,0:T(8,128)} reshape(f32[128,2432]{1,0:T(8,128)S(1)} %gather_fusion) | data formatting | bytes 2490368 | tf_op jit(solution)/shard_map/while/body/eval_jaxpr/gather | solution.py:62
  28.6 18.7 %fusion.27 = f32[16,152,16]{1,2,0:T(8,128)S(1)} fusion(f32[40,152,152]{2,1,0:T(8,128)} %get-tuple-element.173, s32[]{:T(128)S(6)} %select_n.35, f32[16,8,152,16]{3,2,1,0:T(8,128)} %gather.12, f32[16,8]{1,0:T(8,128)S(1)} %compare_convert_fusion.2, f32[16,152,16]{1,2,0:T(8,128)S(1)} %get-tuple-element.155, pred[]{:T(512)S(6)} %compare.8), kind=kOutput, calls=%fused_computation.7.clone.1 | convolution fusion | flops 568193024 | bytes 11518469 | tf_op jit(solution)/shard_map/while/body/eval_jaxpr/cij,tcjr->tir/dot_general | solution.py:65
  47.2 0.7 dynamic_slice.25
  48.6 1.1 select_reduce_fusion.2
  49.8 1.1 gather_fusion
  50.9 5.4 %gather.12 = f32[16,8,152,16]{3,2,1,0:T(8,128)} reshape(f32[128,2432]{1,0:T(8,128)S(1)} %gather_fusion) | data formatting | bytes 2490368 | tf_op jit(solution)/shard_map/while/body/eval_jaxpr/gather | solution.py:62
  56.3 18.7 %fusion.27 = f32[16,152,16]{1,2,0:T(8,128)S(1)} fusion(f32[40,152,152]{2,1,0:T(8,128)} %get-tuple-element.173, s32[]{:T(128)S(6)} %select_n.35, f32[16,8,152,16]{3,2,1,0:T(8,128)} %gather.12, f32[16,8]{1,0:T(8,128)S(1)} %compare_convert_fusion.2, f32[16,152,16]{1,2,0:T(8,128)S(1)} %get-tuple-element.155, pred[]{:T(512)S(6)} %compare.8), kind=kOutput, calls=%fused_computation.7.clone.1 | convolution fusion | flops 568193024 | bytes 11518469 | tf_op jit(solution)/shard_map/while/body/eval_jaxpr/cij,tcjr->tir/dot_general | solution.py:65
  75.0 0.7 dynamic_slice.25
  76.3 1.1 select_reduce_fusion.2
  77.5 1.1 gather_fusion
  78.6 5.4 %gather.12 = f32[16,8,152,16]{3,2,1,0:T(8,128)} reshape(f32[128,2432]{1,0:T(8,128)S(1)} %gather_fusion) | data formatting | bytes 2490368 | tf_op jit(solution)/shard_map/while/body/eval_jaxpr/gather | solution.py:62
  84.0 18.7 %fusion.27 = f32[16,152,16]{1,2,0:T(8,128)S(1)} fusion(f32[40,152,152]{2,1,0:T(8,128)} %get-tuple-element.173, s32[]{:T(128)S(6)} %select_n.35, f32[16,8,152,16]{3,2,1,0:T(8,128)} %gather.12, f32[16,8]{1,0:T(8,128)S(1)} %compare_convert_fusion.2, f32[16,152,16]{1,2,0:T(8,128)S(1)} %get-tuple-element.155, pred[]{:T(512)S(6)} %compare.8), kind=kOutput, calls=%fused_computation.7.clone.1 | convolution fusion | flops 568193024 | bytes 11518469 | tf_op jit(solution)/shard_map/while/body/eval_jaxpr/cij,tcjr->tir/dot_general | solution.py:65
  104.0 1.1 select_reduce_fusion.2
  105.2 1.1 gather_fusion
  106.3 5.4 %gather.12 = f32[16,8,152,16]{3,2,1,0:T(8,128)} reshape(f32[128,2432]{1,0:T(8,128)S(1)} %gather_fusion) | data formatting | bytes 2490368 | tf_op jit(solution)/shard_map/while/body/eval_jaxpr/gather | solution.py:62
  111.7 18.7 %fusion.27 = f32[16,152,16]{1,2,0:T(8,128)S(1)} fusion(f32[40,152,152]{2,1,0:T(8,128)} %get-tuple-element.173, s32[]{:T(128)S(6)} %select_n.35, f32[16,8,152,16]{3,2,1,0:T(8,128)} %gather.12, f32[16,8]{1,0:T(8,128)S(1)} %compare_convert_fusion.2, f32[16,152,16]{1,2,0:T(8,128)S(1)} %get-tuple-element.155, pred[]{:T(512)S(6)} %compare.8), kind=kOutput, calls=%fused_computation.7.clone.1 | convolution fusion | flops 568193024 | bytes 11518469 | tf_op jit(solution)/shard_map/while/body/eval_jaxpr/cij,tcjr->tir/dot_general | solution.py:65
  131.7 1.1 select_reduce_fusion.2
  132.9 1.1 gather_fusion
  134.0 5.4 %gather.12 = f32[16,8,152,16]{3,2,1,0:T(8,128)} reshape(f32[128,2432]{1,0:T(8,128)S(1)} %gather_fusion) | data formatting | bytes 2490368 | tf_op jit(solution)/shard_map/while/body/eval_jaxpr/gather | solution.py:62
  139.4 18.7 %fusion.27 = f32[16,152,16]{1,2,0:T(8,128)S(1)} fusion(f32[40,152,152]{2,1,0:T(8,128)} %get-tuple-element.173, s32[]{:T(128)S(6)} %select_n.35, f32[16,8,152,16]{3,2,1,0:T(8,128)} %gather.12, f32[16,8]{1,0:T(8,128)S(1)} %compare_convert_fusion.2, f32[16,152,16]{1,2,0:T(8,128)S(1)} %get-tuple-element.155, pred[]{:T(512)S(6)} %compare.8), kind=kOutput, calls=%fused_computation.7.clone.1 | convolution fusion | flops 568193024 | bytes 11518469 | tf_op jit(solution)/shard_map/while/body/eval_jaxpr/cij,tcjr->tir/dot_general | solution.py:65
  158.5 1.0 reshape.27
  159.6 18.7 %all-reduce.5.cloned.1.call-done = f32[16,2432]{1,0:T(8,128)} async-done(((f32[16,2432]{1,0:T(8,128)}), f32[16,2432]{1,0:T(8,128)}) %all-reduce.5.cloned.1.call-update) | async-done | bytes 155664 | tf_op jit(solution)/shard_map/psum | solution.py:76
  178.3 1.5 constant_dynamic-slice_fusion
  (38 shorter events, 3.4 us)
Async XLA Ops:
  6.5 1.0 copy-start
  6.5 171.8 %all-reduce.5.cloned.1.call-start = ((), (), s32[]{:S(2)}) async-start(), calls=%async_computation | async-start | bytes 311296 | tf_op jit(solution)/shard_map/psum | solution.py:76
  7.9 11.1 %collective-permute-start = (f32[16,2432]{1,0:T(8,128)S(1)}, f32[16,2432]{1,0:T(8,128)S(1)}, u32[]{:S(2)}, u32[]{:S(2)}) collective-permute-start(f32[16,2432]{1,0:T(8,128)S(1)} %get-tuple-element.91), channel_id=1, source_target_pairs={{0,2},{2,4},{4,6},{6,8},{8,10},{10,12},{12,14},{14,16},{16,18},{18... | collective-permute-start | bytes 466952 | tf_op jit(solution)/shard_map/ppermute | solution.py:21
  10.9 8.6 %collective-permute-start.1 = (f32[16,2432]{1,0:T(8,128)S(1)}, f32[16,2432]{1,0:T(8,128)S(1)}, u32[]{:S(2)}, u32[]{:S(2)}) collective-permute-start(f32[16,2432]{1,0:T(8,128)S(1)} %get-tuple-element.92), channel_id=1, source_target_pairs={{2,0},{4,2},{6,4},{8,6},{10,8},{12,10},{14,12},{16,14},{18,16},{20... | collective-permute-start | bytes 466952 | tf_op jit(solution)/shard_map/ppermute | solution.py:24
Sparse Core Ops, SparseCore 0:
  159.7 18.5 all-reduce.4
where the time goes:
time: 187 us
  matrix products  93.7 us (50%)
  local copies, waits for them, and re-layouts  39.4 us (21%)
  waiting for transfers between devices  22.6 us (12%)
  between operations  13.4 us (7%)
  other arithmetic  7.08 us (4%)
  starting transfers between devices  7.05 us (4%)
  loops' own time  3.54 us (2%)
    dot_general x5, matrix products, class_block(): jnp.einsum('cij,tcjr->tir', blocks, sources, precision=lax.Precision.HIGH...  93.3 us
    gather x10, local copies, waits for them, and re-layouts, class_block(): sources = window[jnp.maximum(chosen, 0)] * present[:, :, None]  32.5 us
    psum x1, waiting for transfers between devices, local(): whole = lax.psum(partial_sum, 'off')  18.7 us
    reduce_max x5, other arithmetic, class_block(): chosen = jnp.max(jnp.where(matches, window_ids[:, :, None], -1), axis=1)  5.54 us
    ppermute x1, starting transfers between devices, padded(): lax.ppermute(lax.slice_in_dim(block, 0, width, axis=dim), axis, backward)  4.06 us
  transfers between devices with their start and end apart: 3, of which 3 were waited for; matrix products, arithmetic and copies ran while one was open for 0% of the time, Pallas kernels for 0%

commit v1 on v0

v1 whole, which is shorter than its diff:
```python
import functools

import jax
import jax.numpy as jnp
from jax import lax
from jax.experimental import pallas as pl
from jax.experimental.pallas import tpu as pltpu
from jax.sharding import PartitionSpec as P

TGT = 16
SPILL = 4
LANES = 128
ROWS = 8
BODY = 64
TAIL = 16
HALF = BODY + TAIL
STEPS = 4
WINDOW = 5
VMEM_LIMIT = 48 * 1024 * 1024
f32, bf16, i32 = jnp.float32, jnp.bfloat16, jnp.int32


def swap_blocks(x, width):
    row = lax.broadcasted_iota(i32, (ROWS, LANES), 0)
    lane = lax.broadcasted_iota(i32, (ROWS, LANES), 1)
    take = functools.partial(jnp.take_along_axis, mode="promise_in_bounds")
    x = take(x, (lane - width * row) & (LANES - 1), axis=1)
    x = take(x, (lane // width - row) & (ROWS - 1), axis=0)
    return take(x, (lane + width * row) & (LANES - 1), axis=1)


def chunk_of(half, at):
    body = BODY // ROWS
    return half * body + at if at < body else 2 * body + half * (TAIL // ROWS) + at - body


def table_kernel(width, octants, slot_hbm, contrib_hbm, right_ref, left_ref, table, slot_ref, contrib_ref, sems):
    copies = [
        pltpu.make_async_copy(slot_hbm, slot_ref, sems.at[0]),
        pltpu.make_async_copy(contrib_hbm, contrib_ref, sems.at[1]),
    ]
    for copy in copies:
        copy.start()
    first = lax.axis_index("dom") * TGT - SPILL
    half = lax.rem(lax.axis_index("off"), 2)
    length = contrib_ref.shape[1]
    table[:ROWS] = jnp.zeros((ROWS, table.shape[1]), f32)
    table[ROWS:TGT, length:] = jnp.zeros((ROWS, table.shape[1] - length), f32)
    table[TGT:] = jnp.zeros((ROWS, table.shape[1]), f32)
    for copy in copies:
        copy.wait()
    table[SPILL : SPILL + TGT, :length] = contrib_ref[:TGT, :]
    for slot in range(TGT, contrib_ref.shape[0]):
        row = lax.rem(slot_ref[slot] - first + octants, octants)
        table[pl.ds(row, 1), :length] += contrib_ref[slot : slot + 1, :]
    for chunk in range(HALF // ROWS):
        lanes = pl.ds(pl.multiple_of(chunk_of(half, chunk) * LANES, LANES), LANES)
        rows = slice(ROWS * chunk, ROWS * (chunk + 1))
        for block in range(3):
            piece = swap_blocks(table[ROWS * block : ROWS * (block + 1), lanes], width)
            if block < 2:
                left_ref[rows, LANES * block : LANES * (block + 1)] = piece
            if block >= 1:
                right_ref[rows, LANES * (block - 1) : LANES * block] = piece


def fill_own(width, table, own_ref):
    for half in range(2):
        for chunk in range(HALF // ROWS):
            at = chunk_of(half, chunk)
            for block in range(3):
                piece = table[ROWS * block : ROWS * (block + 1), LANES * at : LANES * (at + 1)]
                rows, lanes = slice(ROWS * chunk, ROWS * (chunk + 1)), slice(LANES * block, LANES * (block + 1))
                own_ref[half, rows, lanes] = swap_blocks(piece, width)


def halves(x):
    high = x.astype(bf16)
    return high, (x - high.astype(f32)).astype(bf16)


def tail_places():
    source = lax.broadcasted_iota(i32, (2 * LANES, 2 * LANES), 0)
    lane = lax.broadcasted_iota(i32, (2 * LANES, 2 * LANES), 1)
    slot = (lane & (LANES - 1)) // TAIL - BODY // TAIL
    point = lane // LANES * TAIL + lane % TAIL
    wanted = jnp.where(slot == 1, LANES + point, point)
    return jnp.where((slot >= 0) & (slot < 3) & (source == wanted), 1.0, 0.0).astype(bf16)


def fetch(block_hbm, block_ref, sem, begin, end):
    here = pl.ds(begin, end - begin)
    return pltpu.make_async_copy(block_hbm.at[here], block_ref.at[here], sem)


def split_blocks(places, begin, end, block_ref, split_ref):
    points = block_ref.shape[1]
    spare = jnp.zeros((points, 2 * LANES - points), f32)
    lower = lax.broadcasted_iota(i32, (points, LANES), 1) < BODY
    for at in range(begin, end):
        high, low = halves(block_ref[at, :, :LANES])
        rest = jnp.concatenate(halves(jnp.concatenate([block_ref[at, :, LANES:], spare], axis=1)), axis=1)
        tails = jnp.dot(rest, places, preferred_element_type=f32).astype(bf16)
        turned = pltpu.roll(low, BODY, 1)
        split_ref[at, 0, :, :LANES] = jnp.where(lower, high, turned)
        split_ref[at, 0, :, LANES:] = jnp.where(lower, high, tails[:, :LANES])
        split_ref[at, 1, :, :LANES] = jnp.where(lower, turned, high)
        split_ref[at, 1, :, LANES:] = jnp.where(lower, pltpu.roll(high, BODY, 1), tails[:, LANES:])


def find_targets(width, octants, src_ref, class_ref, mask_ref, place_ref):
    count, targets = mask_ref.shape[0], src_ref.shape[0]
    first_class = lax.axis_index("off") * count
    first = lax.axis_index("dom") * TGT
    reach = TGT - SPILL
    target = lax.broadcasted_iota(i32, src_ref.shape, 0)
    offset = lax.rem(src_ref[...] - (first + target) + reach + octants, octants)
    named = class_ref[...] - first_class
    known = (named >= 0) & (named < count)
    code = jnp.where(known, named * 32 + offset, -1).astype(f32)
    owner = lax.broadcasted_iota(i32, (targets, targets * width), 1) // width
    spread = (owner == lax.broadcasted_iota(i32, owner.shape, 0)).astype(f32)
    codes = lax.dot_general(
        code, spread, (((0,), (0,)), ((), ())), precision=lax.Precision.HIGHEST, preferred_element_type=f32
    ).astype(i32)
    for at in range(count):
        found = jnp.where((codes >> 5) == at, codes & 31, -1)
        found = jnp.max(found, axis=0, keepdims=True)
        mask_ref[at : at + 1, :] = (found >= 0).astype(f32)
        best = jnp.max(found, axis=1, keepdims=True)
        shift, turns = jnp.maximum(best[0, 0], 0), LANES // width
        place_ref[at] = lax.rem(shift, turns) * WINDOW + lax.div(shift, turns)


def early_share():
    return jnp.clip(STEPS - lax.axis_index("dom") * 3 // 2, 0, STEPS)


def early_kernel(width, bounds, block_hbm, table, sent_ref, split_ref, own_ref, copied_ref, block_ref, sems):
    copied_ref[...] = sent_ref[...]
    share = early_share()
    copies = [fetch(block_hbm, block_ref, sems.at[step], *bounds[step : step + 2]) for step in range(STEPS)]
    for step in range(STEPS):
        pl.when(step < share)(copies[step].start)

    @pl.when(share > 0)
    def _():
        fill_own(width, table, own_ref)
        places = tail_places()
        for step in range(STEPS):

            @pl.when(step < share)
            def _():
                copies[step].wait()
                split_blocks(places, bounds[step], bounds[step + 1], block_ref, split_ref)


def late_kernel(
    width, octants, bounds, src_hbm, class_hbm, block_hbm, table, _split, _own, split_ref, own_ref, mask_ref, place_ref,
    src_ref, class_ref, block_ref, sems, table_sems
):
    share = early_share()
    tables = [
        pltpu.make_async_copy(src_hbm, src_ref, table_sems.at[0]),
        pltpu.make_async_copy(class_hbm, class_ref, table_sems.at[1]),
    ]
    for copy in tables:
        copy.start()
    steps = len(bounds) - 1
    copies = [fetch(block_hbm, block_ref, sems.at[step], *bounds[step : step + 2]) for step in range(steps)]
    for step in range(steps):
        if step < STEPS:
            pl.when(step >= share)(copies[step].start)
        else:
            copies[step].start()
    pl.when(share == 0)(lambda: fill_own(width, table, own_ref))
    for copy in tables:
        copy.wait()
    find_targets(width, octants, src_ref, class_ref, mask_ref, place_ref)
    places = tail_places()
    for step in range(steps):

        def one_step(step=step):
            copies[step].wait()
            split_blocks(places, bounds[step], bounds[step + 1], block_ref, split_ref)

        if step < STEPS:
            pl.when(step >= share)(one_step)
        else:
            one_step()


def edge_kernel(side, sent_ref, own_ref, *refs):
    half = lax.rem(lax.axis_index("off"), 2)
    near = LANES * (1 - side)
    edge_ref = refs[-1]
    own = own_ref[half, :, 2 * LANES * side : 2 * LANES * side + LANES]
    for at in range(0, 2 * LANES, LANES):
        block = sent_ref[:, at : at + LANES]
        edge_ref[:, at : at + LANES] = block + own if at == near else block


def turn_kernel(width, other, side, edge_ref, own_ref, *refs):
    half = lax.rem(lax.axis_index("off") + other, 2)
    shifted = refs[-1]
    blocks = [edge_ref[:, :LANES], edge_ref[:, LANES:]]
    if side == 0:
        blocks.append(own_ref[half, :, LANES : 2 * LANES])
    stacks = [jnp.concatenate(halves(block), axis=0) for block in blocks]
    lane = lax.broadcasted_iota(i32, stacks[0].shape, 1)
    for turn in range(LANES // width):
        tiles = [pltpu.roll(stack, LANES - width * turn, 1) for stack in stacks] if turn else stacks
        kept = lane < LANES - width * turn
        row = turn * WINDOW
        if side == 0:
            shifted[row] = jnp.where(kept, tiles[0], tiles[1]) if turn else tiles[0]
            shifted[row + 1] = jnp.where(kept, tiles[1], tiles[2]) if turn else tiles[1]
            shifted[row + 2] = tiles[2]
        else:
            if turn:
                shifted[row + 2] = jnp.where(kept, shifted[row + 2], tiles[0])
            shifted[row + 3] = jnp.where(kept, tiles[0], tiles[1]) if turn else tiles[0]
            if not turn:
                shifted[row + 4] = tiles[1]


def multiply_kernel(width, other, split_ref, mask_ref, place_ref, shifted, *refs):
    half = lax.rem(lax.axis_index("off") + other, 2)
    points = split_ref.shape[2]
    span = TGT * width
    if other:
        sum_ref, *out_refs = refs
    else:
        (sum_ref,) = refs
    total = sum_ref[...] if other else jnp.zeros((points, span), f32)
    none = jnp.zeros((TAIL, span), bf16)
    for at in range(mask_ref.shape[0]):
        place = place_ref[at]
        here = mask_ref[at : at + 1, :].astype(bf16)
        both = jnp.concatenate([shifted[place], shifted[place + 1]], axis=1) * here
        high, high_tail, low, low_tail = both[:BODY], both[BODY:HALF], both[HALF : HALF + BODY], both[HALF + BODY :]
        depth = [high, high, low, high_tail, high_tail, low_tail, none]
        total += jnp.dot(split_ref[at, half], jnp.concatenate(depth, axis=0), preferred_element_type=f32)
    if not other:
        sum_ref[...] = total
        return
    shares = len(out_refs)
    lanes = span // shares
    me = lax.axis_index("off")
    for step, out_ref in enumerate(out_refs):
        piece = total[:, :lanes]
        for share in range(1, shares):
            mine = lax.rem(me + step, shares) == share
            piece = jnp.where(mine, total[:, share * lanes : (share + 1) * lanes], piece)
        out_ref[...] = piece


def finish_kernel(width, *refs):
    *in_refs, out_ref = refs
    total = in_refs[0][...]
    for ref in in_refs[1:]:
        total += ref[...]
    lanes = total.shape[1]
    if lanes < LANES:
        total = jnp.concatenate([total, jnp.zeros((total.shape[0], LANES - lanes), f32)], axis=1)
    for tile in range(total.shape[1] // LANES):
        rows = slice(ROWS * tile, min(ROWS * (tile + 1), out_ref.shape[0]))
        for chunk in range(total.shape[0] // ROWS):
            piece = total[ROWS * chunk : ROWS * (chunk + 1), LANES * tile : LANES * (tile + 1)]
            piece = swap_blocks(piece, width)
            out_ref[rows, LANES * chunk : LANES * (chunk + 1)] = piece[: rows.stop - rows.start]


def local(contrib, slot_octant, vlist_src, vlist_class, translation):
    count = lax.axis_size("dom")
    shares = lax.axis_size("off")
    octants = TGT * count
    classes, points, _ = translation.shape
    width = contrib.shape[1] // points
    span = TGT * width
    vmem = pl.BlockSpec(memory_space=pltpu.VMEM)
    smem = pl.BlockSpec(memory_space=pltpu.SMEM)
    hbm = pl.BlockSpec(memory_space=pltpu.HBM)
    params = pltpu.CompilerParams(vmem_limit_bytes=VMEM_LIMIT)

    def call(kernel, name, out_shape, in_specs, scratch_shapes=(), **options):
        run = pl.pallas_call(
            kernel,
            out_shape=out_shape,
            in_specs=in_specs,
            out_specs=jax.tree.map(lambda x: smem if x.shape == (classes,) else vmem, out_shape),
            scratch_shapes=scratch_shapes,
            compiler_params=params,
            name=name,
            **options,
        )
        places = [pltpu.VMEM if spec is vmem else pltpu.SMEM if spec is smem else pltpu.HBM for spec in in_specs]
        return lambda *operands: run(*map(pltpu.with_memory_space_constraint, operands, places))

    half_shape = pltpu.VMEM((HALF, span), f32)
    to_right, to_left, table = call(
        functools.partial(table_kernel, width, octants),
        "table",
        [half_shape, half_shape, pltpu.VMEM((TGT + 2 * SPILL, 2 * HALF * width), f32)],
        [hbm] * 2,
        [pltpu.SMEM(slot_octant.shape, i32), pltpu.VMEM(contrib.shape, f32), pltpu.SemaphoreType.DMA((2,))],
    )(slot_octant, contrib)

    forward = [(i, (i + 1) % count) for i in range(count)]
    backward = [(target, source) for source, target in forward]
    low = lax.ppermute(to_right, "dom", forward)

    step = classes * 7 // 40
    bounds = [step * at for at in range(STEPS + 1)]
    bounds += [(bounds[-1] + classes) // 2, classes]
    split_shape = pltpu.VMEM((classes, 2, points, 2 * LANES), bf16)
    own_shape = pltpu.VMEM((2, HALF, 3 * LANES), f32)
    blocks = pltpu.VMEM(translation.shape, f32)
    split, own, to_left = call(
        functools.partial(early_kernel, width, bounds),
        "early",
        [split_shape, own_shape, half_shape],
        [hbm, vmem, vmem],
        [blocks, pltpu.SemaphoreType.DMA((STEPS,))],
    )(translation, table, to_left)
    high = lax.ppermute(to_left, "dom", backward)
    tables = [pltpu.VMEM(vlist_src.shape, i32), pltpu.VMEM(vlist_class.shape, i32)]
    split, own, *facts = call(
        functools.partial(late_kernel, width, octants, bounds),
        "late",
        [split_shape, own_shape, pltpu.VMEM((classes, span), f32), pltpu.SMEM((classes,), i32)],
        [hbm] * 3 + [vmem] * 3,
        tables + [blocks, pltpu.SemaphoreType.DMA((len(bounds) - 1,)), pltpu.SemaphoreType.DMA((2,))],
        input_output_aliases={4: 0, 5: 1},
    )(vlist_src, vlist_class, translation, table, split, own)
    facts.insert(0, split)

    twins = [(i, i ^ 1) for i in range(shares)]
    turned_shape = pltpu.VMEM((LANES // width * WINDOW, 2 * HALF, LANES), bf16)

    def turned(other, side, edge, *before):
        return call(
            functools.partial(turn_kernel, width, other, side),
            ("left" if side == 0 else "right") + "_turns",
            turned_shape,
            [vmem] * (2 + len(before)),
            **({"input_output_aliases": {2: 0}} if before else {}),
        )(edge, own, *before)

    def edge(side, sent, after, spec):
        return call(functools.partial(edge_kernel, side), "edge", half_shape, [vmem] * 2 + [spec])(sent, own, after)

    left = edge(0, low, facts[2], smem)
    left_other = lax.ppermute(left, "off", twins)
    window = turned(0, 0, left)
    right = edge(1, high, window, vmem)
    right_other = lax.ppermute(right, "off", twins)
    window = turned(0, 1, right, window)
    total = call(
        functools.partial(multiply_kernel, width, 0), "first", pltpu.VMEM((points, span), f32), [vmem, vmem, smem, vmem]
    )(*facts, window)
    window = turned(1, 1, right_other, turned(1, 0, left_other))
    shares_out = call(
        functools.partial(multiply_kernel, width, 1),
        "second",
        [pltpu.VMEM((points, span // shares), f32)] * shares,
        [vmem, vmem, smem, vmem, vmem],
    )(*facts, window, total)

    pieces = [shares_out[0]]
    for step in range(1, shares):
        pairs = [(i, (i + step) % shares) for i in range(shares)]
        pieces.append(lax.ppermute(shares_out[step], "off", pairs))
    return call(
        functools.partial(finish_kernel, width),
        "finish",
        jax.ShapeDtypeStruct((TGT // shares, contrib.shape[1]), f32),
        [vmem] * shares,
    )(*pieces)


def solution(mesh):
    return jax.shard_map(
        local,
        mesh=mesh,
        in_specs=(P("dom", None), P("dom"), P("dom", None), P("dom", None), P("off", None, None)),
        out_specs=P(("dom", "off"), None),
        check_vma=False,
    )
```

time: 187 us -> 17 us (0.09)
  matrix products: 93.7 us -> 0 us
  local copies, waits for them, and re-layouts: 39.4 us -> 0 us
  waiting for transfers between devices: 22.6 us -> 1.46 us
  between operations: 13.4 us -> 0.11 us
  Pallas kernels: 0 us -> 10.1 us
  other arithmetic: 7.08 us -> 0 us
  loops' own time: 3.54 us -> 0 us
  starting transfers between devices: 7.05 us -> 5.12 us
    dot_general x6 -> x0, matrix products: 93.7 us -> none  [the longest x5 93.3 us: class_block(): jnp.einsum('cij,tcjr->tir', blocks, sources, precision=lax.Precision.HIGH...]
    gather x10 -> x0, local copies, waits for them, and re-layouts: 32.5 us -> none  [class_block(): sources = window[jnp.maximum(chosen, 0)] * present[:, :, None]]
    psum x1 -> x0, waiting for transfers between devices: 18.7 us -> none  [local(): whole = lax.psum(partial_sum, 'off')]
    pallas_call x0 -> x12, Pallas kernels: none -> 10.1 us  [call(): run(*map(pltpu.with_memory_space_constraint, operands, places))]
    reduce_max x5 -> x0, other arithmetic: 5.54 us -> none  [class_block(): chosen = jnp.max(jnp.where(matches, window_ids[:, :, None], -1), axis=1)]
    dynamic_slice x6 -> x0, local copies, waits for them, and re-layouts: 4.77 us -> none  [the longest x5 3.25 us: local(): lax.scan(class_block, jnp.zeros((targets, E, R), jnp.float32), jnp.arange...]
    another operation x1 -> x0, loops' own time: 3.54 us -> none  [local(): lax.scan(class_block, jnp.zeros((targets, E, R), jnp.float32), jnp.arange...]
    ppermute x2 -> x5, waiting for transfers between devices: 3.8 us -> 1.46 us  [the longest x1 1.02 us: local(): pieces.append(lax.ppermute(shares_out[step], 'off', pairs))]
  transfers between devices with their start and end apart: 3 -> 5, of which waited for: 3 -> 3; matrix products, arithmetic and copies ran while one was open for 0% -> 0% of each run, Pallas kernels for 0% -> 40%
where the time goes in v1:
time: 17 us; the launch traced here: 16.8 us
  Pallas kernels  10.1 us (59%)
  starting transfers between devices  5.12 us (30%)
  waiting for transfers between devices  1.46 us (9%)
    pallas_call x12, Pallas kernels, call(): run(*map(pltpu.with_memory_space_constraint, operands, places))  10.1 us
    ppermute x1, starting transfers between devices, local(): low = lax.ppermute(to_right, 'dom', forward)  2.99 us
    ppermute x1, starting transfers between devices, local(): high = lax.ppermute(to_left, 'dom', backward)  1.43 us
    ppermute x1, waiting for transfers between devices, local(): pieces.append(lax.ppermute(shares_out[step], 'off', pairs))  1.02 us
  transfers between devices with their start and end apart: 5, of which 3 were waited for; matrix products, arithmetic and copies ran while one was open for 0% of the time, Pallas kernels for 40%

profile of v1, /device:TPU:0, one launch (start us, length us, event | category | flops | bytes accessed | tf_op | source)
XLA Modules:
  0.0 16.8 jit_solution(1980579261044898842)
XLA Ops:
  0.0 1.2 %table.1 = (f32[80,256]{1,0:T(8,128)S(1)}, f32[80,256]{1,0:T(8,128)S(1)}, f32[24,2560]{1,0:T(8,128)S(1)}) custom-call(s32[24]{0:T(128)} %slot_hbm.1, f32[24,2432]{1,0:T(8,128)} %contrib_hbm.1), custom_call_target="tpu_custom_call" | custom-call | tf_op jit(solution)/shard_map/table/pallas_call | solution.py:298
  1.2 3.0 %collective-permute-start.1 = (f32[80,256]{1,0:T(8,128)S(1)}, f32[80,256]{1,0:T(8,128)S(1)}, u32[]{:S(2)}, u32[]{:S(2)}) collective-permute-start(f32[80,256]{1,0:T(8,128)S(1)} %get-tuple-element.26), channel_id=1, source_target_pairs={{0,2},{2,4},{4,6},{6,8},{8,10},{10,12},{12,14},{14,16},{16,18},{18... | collective-permute-start | bytes 245768 | tf_op jit(solution)/shard_map/ppermute | solution.py:311
  4.2 2.7 %early.1 = (bf16[40,2,152,256]{3,2,1,0:T(8,128)(2,1)S(1)}, f32[2,80,384]{2,1,0:T(8,128)S(1)}, f32[80,256]{1,0:T(8,128)S(1)}) custom-call(f32[40,152,152]{2,1,0:T(8,128)} %block_hbm.3, f32[24,2560]{1,0:T(8,128)S(1)} %get-tuple-element.17.table, f32[80,256]{1,0:T(8,128)S(1)} %get-tuple-element.18.sent_ref), custom_call_target="tpu_custom_call" | custom-call | tf_op jit(solution)/shard_map/early/pallas_call | solution.py:298
  6.9 1.4 %collective-permute-start = (f32[80,256]{1,0:T(8,128)S(1)}, f32[80,256]{1,0:T(8,128)S(1)}, u32[]{:S(2)}, u32[]{:S(2)}) collective-permute-start(f32[80,256]{1,0:T(8,128)S(1)} %get-tuple-element.24), channel_id=1, source_target_pairs={{2,0},{4,2},{6,4},{8,6},{10,8},{12,10},{14,12},{16,14},{18,16},{20... | collective-permute-start | bytes 245768 | tf_op jit(solution)/shard_map/ppermute | solution.py:326
  8.3 2.2 %late.1 = (bf16[40,2,152,256]{3,2,1,0:T(8,128)(2,1)S(1)}, f32[2,80,384]{2,1,0:T(8,128)S(1)}, f32[40,256]{1,0:T(8,128)S(1)}, s32[40]{0:T(128)S(4)}) custom-call(s32[16,40]{1,0:T(8,128)} %src_hbm.1, s32[16,40]{1,0:T(8,128)} %class_hbm.1, f32[40,152,152]{2,1,0:T(8,128)} %block_hbm.3, ...), custom_call_target="tpu_custom_call", output_to_operand_aliasing={{0}: (4, {}), {1}: (5, {})} | custom-call | tf_op jit(solution)/shard_map/late/pallas_call | solution.py:298
  10.6 0.2 %collective-permute-done.1.sent_ref = f32[80,256]{1,0:T(8,128)S(1)} collective-permute-done((f32[80,256]{1,0:T(8,128)S(1)}, f32[80,256]{1,0:T(8,128)S(1)}, u32[]{:S(2)}, u32[]{:S(2)}) %collective-permute-start.1) | collective-permute-done | bytes 81952 | tf_op jit(solution)/shard_map/ppermute | solution.py:311
  10.8 0.1 collective-permute-start.3
  10.8 0.3 %left_turns.2.refs_0_ = bf16[40,160,128]{2,1,0:T(8,128)(2,1)S(1)} custom-call(f32[80,256]{1,0:T(8,128)S(1)} %edge.2.edge_ref, f32[2,80,384]{2,1,0:T(8,128)S(1)} %get-tuple-element.25.own_ref), custom_call_target="tpu_custom_call" | custom-call | tf_op jit(solution)/shard_map/left_turns/pallas_call | solution.py:298
  11.1 0.3 %collective-permute-done.sent_ref = f32[80,256]{1,0:T(8,128)S(1)} collective-permute-done((f32[80,256]{1,0:T(8,128)S(1)}, f32[80,256]{1,0:T(8,128)S(1)}, u32[]{:S(2)}, u32[]{:S(2)}) %collective-permute-start) | collective-permute-done | bytes 81952 | tf_op jit(solution)/shard_map/ppermute | solution.py:326
  11.4 0.3 %collective-permute-start.2 = (f32[80,256]{1,0:T(8,128)S(1)}, f32[80,256]{1,0:T(8,128)S(1)}, u32[]{:S(2)}, u32[]{:S(2)}) collective-permute-start(f32[80,256]{1,0:T(8,128)S(1)} %edge.3.edge_ref), channel_id=1, source_target_pairs={{0,1},{1,0},{2,3},{3,2},{4,5},{5,4},{6,7},{7,6},{8,9},{9,8},{10,11... | collective-permute-start | bytes 245768 | tf_op jit(solution)/shard_map/ppermute | solution.py:357
  11.7 0.2 %right_turns.3.shifted = bf16[40,160,128]{2,1,0:T(8,128)(2,1)S(1)} custom-call(f32[80,256]{1,0:T(8,128)S(1)} %edge.3.edge_ref, f32[2,80,384]{2,1,0:T(8,128)S(1)} %get-tuple-element.25.own_ref, bf16[40,160,128]{2,1,0:T(8,128)(2,1)S(1)} %left_turns.2.refs_0_), custom_call_target="tpu_custom_call", output_to_operand_aliasing={{}: (2, {})} | custom-call | tf_op jit(solution)/shard_map/right_turns/pallas_call | solution.py:298
  12.0 1.1 %first.1.refs_0_ = f32[152,256]{1,0:T(8,128)S(1)} custom-call(bf16[40,2,152,256]{3,2,1,0:T(8,128)(2,1)S(1)} %get-tuple-element.21.split_ref, f32[40,256]{1,0:T(8,128)S(1)} %get-tuple-element.22.mask_ref, s32[40]{0:T(128)S(4)} %get-tuple-element.23.refs_0_.place_ref, bf16[40,160,128]{2,1,0:T(8,128)(2,1)S(1)} %right_turns.3.shifted), custom_call_target="tpu_custom_call" | custom-call | tf_op jit(solution)/shard_map/first/pallas_call | solution.py:298
  13.0 0.0 collective-permute-done.3.edge_ref
  13.0 0.3 %left_turns.3.refs_0_ = bf16[40,160,128]{2,1,0:T(8,128)(2,1)S(1)} custom-call(f32[80,256]{1,0:T(8,128)S(1)} %collective-permute-done.3.edge_ref, f32[2,80,384]{2,1,0:T(8,128)S(1)} %get-tuple-element.25.own_ref), custom_call_target="tpu_custom_call" | custom-call | tf_op jit(solution)/shard_map/left_turns/pallas_call | solution.py:298
  13.3 0.0 collective-permute-done.2.edge_ref
  13.3 0.2 %right_turns.2.shifted = bf16[40,160,128]{2,1,0:T(8,128)(2,1)S(1)} custom-call(f32[80,256]{1,0:T(8,128)S(1)} %collective-permute-done.2.edge_ref, f32[2,80,384]{2,1,0:T(8,128)S(1)} %get-tuple-element.25.own_ref, bf16[40,160,128]{2,1,0:T(8,128)(2,1)S(1)} %left_turns.3.refs_0_), custom_call_target="tpu_custom_call", output_to_operand_aliasing={{}: (2, {})} | custom-call | tf_op jit(solution)/shard_map/right_turns/pallas_call | solution.py:298
  13.6 1.1 %second.1 = (f32[152,128]{1,0:T(8,128)S(1)}, f32[152,128]{1,0:T(8,128)S(1)}) custom-call(bf16[40,2,152,256]{3,2,1,0:T(8,128)(2,1)S(1)} %get-tuple-element.21.split_ref, f32[40,256]{1,0:T(8,128)S(1)} %get-tuple-element.22.mask_ref, s32[40]{0:T(128)S(4)} %get-tuple-element.23.refs_0_.place_ref, bf16[40,160,128]{2,1,0:T(8,128)(2,1)S(1)} %right_turns.2.shifted, ...), custom_call_target="tpu_custom_call" | custom-call | tf_op jit(solution)/shard_map/second/pallas_call | solution.py:298
  14.7 0.3 %collective-permute-start.4 = (f32[152,128]{1,0:T(8,128)S(1)}, f32[152,128]{1,0:T(8,128)S(1)}, u32[]{:S(2)}, u32[]{:S(2)}) collective-permute-start(f32[152,128]{1,0:T(8,128)S(1)} %get-tuple-element.28), channel_id=1, source_target_pairs={{0,1},{1,0},{2,3},{3,2},{4,5},{5,4},{6,7},{7,6},{8,9},{9,8},{10,11... | collective-permute-start | bytes 233480 | tf_op jit(solution)/shard_map/ppermute | solution.py:373
  15.0 1.0 %collective-permute-done.4.refs_1_ = f32[152,128]{1,0:T(8,128)S(1)} collective-permute-done((f32[152,128]{1,0:T(8,128)S(1)}, f32[152,128]{1,0:T(8,128)S(1)}, u32[]{:S(2)}, u32[]{:S(2)}) %collective-permute-start.4) | collective-permute-done | bytes 77856 | tf_op jit(solution)/shard_map/ppermute | solution.py:373
  16.0 0.8 %finish.1 = f32[8,2432]{1,0:T(8,128)} custom-call(f32[152,128]{1,0:T(8,128)S(1)} %get-tuple-element.27.refs_0_, f32[152,128]{1,0:T(8,128)S(1)} %collective-permute-done.4.refs_1_), custom_call_target="tpu_custom_call" | custom-call | tf_op jit(solution)/shard_map/finish/pallas_call | solution.py:298
  (2 shorter events, 0.0 us)
Async XLA Ops:
  1.2 9.5 %collective-permute-start.1 = (f32[80,256]{1,0:T(8,128)S(1)}, f32[80,256]{1,0:T(8,128)S(1)}, u32[]{:S(2)}, u32[]{:S(2)}) collective-permute-start(f32[80,256]{1,0:T(8,128)S(1)} %get-tuple-element.26), channel_id=1, source_target_pairs={{0,2},{2,4},{4,6},{6,8},{8,10},{10,12},{12,14},{14,16},{16,18},{18... | collective-permute-start | bytes 245768 | tf_op jit(solution)/shard_map/ppermute | solution.py:311
  6.9 4.5 %collective-permute-start = (f32[80,256]{1,0:T(8,128)S(1)}, f32[80,256]{1,0:T(8,128)S(1)}, u32[]{:S(2)}, u32[]{:S(2)}) collective-permute-start(f32[80,256]{1,0:T(8,128)S(1)} %get-tuple-element.24), channel_id=1, source_target_pairs={{2,0},{4,2},{6,4},{8,6},{10,8},{12,10},{14,12},{16,14},{18,16},{20... | collective-permute-start | bytes 245768 | tf_op jit(solution)/shard_map/ppermute | solution.py:326
  10.8 2.3 %collective-permute-start.3 = (f32[80,256]{1,0:T(8,128)S(1)}, f32[80,256]{1,0:T(8,128)S(1)}, u32[]{:S(2)}, u32[]{:S(2)}) collective-permute-start(f32[80,256]{1,0:T(8,128)S(1)} %edge.2.edge_ref), channel_id=1, source_target_pairs={{0,1},{1,0},{2,3},{3,2},{4,5},{5,4},{6,7},{7,6},{8,9},{9,8},{10,11... | collective-permute-start | bytes 245768 | tf_op jit(solution)/shard_map/ppermute | solution.py:354
  11.4 1.9 %collective-permute-start.2 = (f32[80,256]{1,0:T(8,128)S(1)}, f32[80,256]{1,0:T(8,128)S(1)}, u32[]{:S(2)}, u32[]{:S(2)}) collective-permute-start(f32[80,256]{1,0:T(8,128)S(1)} %edge.3.edge_ref), channel_id=1, source_target_pairs={{0,1},{1,0},{2,3},{3,2},{4,5},{5,4},{6,7},{7,6},{8,9},{9,8},{10,11... | collective-permute-start | bytes 245768 | tf_op jit(solution)/shard_map/ppermute | solution.py:357
  14.7 1.3 %collective-permute-start.4 = (f32[152,128]{1,0:T(8,128)S(1)}, f32[152,128]{1,0:T(8,128)S(1)}, u32[]{:S(2)}, u32[]{:S(2)}) collective-permute-start(f32[152,128]{1,0:T(8,128)S(1)} %get-tuple-element.28), channel_id=1, source_target_pairs={{0,1},{1,0},{2,3},{3,2},{4,5},{5,4},{6,7},{7,6},{8,9},{9,8},{10,11... | collective-permute-start | bytes 233480 | tf_op jit(solution)/shard_map/ppermute | solution.py:373

commit v2 on v1

--- a/solution.py
+++ b/solution.py
@@ -34,27 +34,54 @@
     return half * body + at if at < body else 2 * body + half * (TAIL // ROWS) + at - body
 
 
-def table_kernel(width, octants, slot_hbm, contrib_hbm, right_ref, left_ref, table, slot_ref, contrib_ref, sems):
-    copies = [
-        pltpu.make_async_copy(slot_hbm, slot_ref, sems.at[0]),
-        pltpu.make_async_copy(contrib_hbm, contrib_ref, sems.at[1]),
+def add_spill(octants, slot_ref, contrib_ref, table):
+    first = lax.axis_index("dom") * TGT - SPILL
+    for slot in range(TGT, contrib_ref.shape[0]):
+        row = lax.rem(slot_ref[slot] - first + octants, octants)
+        table[pl.ds(row, 1), :] += contrib_ref[slot : slot + 1, :]
+
+
+def table_kernel(width, octants, slot_hbm, contrib_hbm, right_ref, left_ref, slot_ref, contrib_ref, table, sems):
+    half = lax.rem(lax.axis_index("off"), 2)
+    slots = contrib_ref.shape[0]
+    body, tail = BODY // ROWS * LANES, TAIL // ROWS * LANES
+    last = contrib_hbm.shape[1] - 2 * body - tail
+    copies = [pltpu.make_async_copy(slot_hbm, slot_ref, sems.at[0])]
+    for row in range(0, slots, ROWS):
+        copies.append(
+            pltpu.make_async_copy(
+                contrib_hbm.at[pl.ds(row, ROWS), pl.ds(pl.multiple_of(half * body, LANES), body)],
+                contrib_ref.at[pl.ds(row, ROWS), pl.ds(0, body)],
+                sems.at[1 + row // ROWS],
+            )
+        )
+    tails = [
+        pltpu.make_async_copy(
+            contrib_hbm.at[:, pl.ds(2 * body + side * tail, length)],
+            contrib_ref.at[:, pl.ds(body, length)],
+            sems.at[1 + slots // ROWS],
+        )
+        for side, length in enumerate((tail, last))
     ]
     for copy in copies:
         copy.start()
-    first = lax.axis_index("dom") * TGT - SPILL
-    half = lax.rem(lax.axis_index("off"), 2)
-    length = contrib_ref.shape[1]
+    for side, copy in enumerate(tails):
+        pl.when(half == side)(copy.start)
     table[:ROWS] = jnp.zeros((ROWS, table.shape[1]), f32)
-    table[ROWS:TGT, length:] = jnp.zeros((ROWS, table.shape[1] - length), f32)
     table[TGT:] = jnp.zeros((ROWS, table.shape[1]), f32)
+
+    @pl.when(half == 1)
+    def _():
+        contrib_ref[:, body + last :] = jnp.zeros((slots, tail - last), f32)
+
     for copy in copies:
         copy.wait()
-    table[SPILL : SPILL + TGT, :length] = contrib_ref[:TGT, :]
-    for slot in range(TGT, contrib_ref.shape[0]):
-        row = lax.rem(slot_ref[slot] - first + octants, octants)
-        table[pl.ds(row, 1), :length] += contrib_ref[slot : slot + 1, :]
+    for side, copy in enumerate(tails):
+        pl.when(half == side)(copy.wait)
+    table[SPILL : SPILL + TGT, :] = contrib_ref[:TGT, :]
+    add_spill(octants, slot_ref, contrib_ref, table)
     for chunk in range(HALF // ROWS):
-        lanes = pl.ds(pl.multiple_of(chunk_of(half, chunk) * LANES, LANES), LANES)
+        lanes = slice(LANES * chunk, LANES * (chunk + 1))
         rows = slice(ROWS * chunk, ROWS * (chunk + 1))
         for block in range(3):
             piece = swap_blocks(table[ROWS * block : ROWS * (block + 1), lanes], width)
@@ -64,13 +91,30 @@
                 right_ref[rows, LANES * (block - 1) : LANES * block] = piece
 
 
-def fill_own(width, table, own_ref):
+def fetch_own(slot_hbm, contrib_hbm, slot_ref, contrib_ref, _table, sems):
+    return [
+        pltpu.make_async_copy(slot_hbm, slot_ref, sems.at[0]),
+        pltpu.make_async_copy(contrib_hbm, contrib_ref, sems.at[1]),
+    ]
+
+
+def fill_own(width, octants, copies, slot_ref, contrib_ref, table, own_ref):
+    for copy in copies:
+        copy.wait()
+    table[:ROWS] = jnp.zeros((ROWS, table.shape[1]), f32)
+    table[TGT:] = jnp.zeros((ROWS, table.shape[1]), f32)
+    table[SPILL : SPILL + TGT, :] = contrib_ref[:TGT, :]
+    add_spill(octants, slot_ref, contrib_ref, table)
     for half in range(2):
         for chunk in range(HALF // ROWS):
             at = chunk_of(half, chunk)
+            rows = slice(ROWS * chunk, ROWS * (chunk + 1))
             for block in range(3):
+                lanes = slice(LANES * block, LANES * (block + 1))
+                if LANES * at >= table.shape[1]:
+                    own_ref[half, rows, lanes] = jnp.zeros((ROWS, LANES), f32)
+                    continue
                 piece = table[ROWS * block : ROWS * (block + 1), LANES * at : LANES * (at + 1)]
-                rows, lanes = slice(ROWS * chunk, ROWS * (chunk + 1)), slice(LANES * block, LANES * (block + 1))
                 own_ref[half, rows, lanes] = swap_blocks(piece, width)
 
 
@@ -136,16 +180,19 @@
     return jnp.clip(STEPS - lax.axis_index("dom") * 3 // 2, 0, STEPS)
 
 
-def early_kernel(width, bounds, block_hbm, table, sent_ref, split_ref, own_ref, copied_ref, block_ref, sems):
-    copied_ref[...] = sent_ref[...]
+def early_kernel(
+    width, octants, bounds, slot_hbm, contrib_hbm, block_hbm, _sent, split_ref, own_ref, _copied, block_ref, sems, *parts
+):
     share = early_share()
     copies = [fetch(block_hbm, block_ref, sems.at[step], *bounds[step : step + 2]) for step in range(STEPS)]
-    for step in range(STEPS):
-        pl.when(step < share)(copies[step].start)
+    own_copies = fetch_own(slot_hbm, contrib_hbm, *parts)
 
     @pl.when(share > 0)
     def _():
-        fill_own(width, table, own_ref)
+        for copy in own_copies:
+            copy.start()
+        for step in range(STEPS):
+            pl.when(step < share)(copies[step].start)
         places = tail_places()
         for step in range(STEPS):
 
@@ -154,10 +201,12 @@
                 copies[step].wait()
                 split_blocks(places, bounds[step], bounds[step + 1], block_ref, split_ref)
 
+        fill_own(width, octants, own_copies, *parts[:3], own_ref)
+
 
 def late_kernel(
-    width, octants, bounds, src_hbm, class_hbm, block_hbm, table, _split, _own, split_ref, own_ref, mask_ref, place_ref,
-    src_ref, class_ref, block_ref, sems, table_sems
+    width, octants, bounds, src_hbm, class_hbm, slot_hbm, contrib_hbm, block_hbm, _split, _own,
+    split_ref, own_ref, mask_ref, place_ref, src_ref, class_ref, block_ref, sems, table_sems, *parts
 ):
     share = early_share()
     tables = [
@@ -166,6 +215,9 @@
     ]
     for copy in tables:
         copy.start()
+    own_copies = fetch_own(slot_hbm, contrib_hbm, *parts)
+    for copy in own_copies:
+        pl.when(share == 0)(copy.start)
     steps = len(bounds) - 1
     copies = [fetch(block_hbm, block_ref, sems.at[step], *bounds[step : step + 2]) for step in range(steps)]
     for step in range(steps):
@@ -173,7 +225,6 @@
             pl.when(step >= share)(copies[step].start)
         else:
             copies[step].start()
-    pl.when(share == 0)(lambda: fill_own(width, table, own_ref))
     for copy in tables:
         copy.wait()
     find_targets(width, octants, src_ref, class_ref, mask_ref, place_ref)
@@ -188,6 +239,7 @@
             pl.when(step >= share)(one_step)
         else:
             one_step()
+    pl.when(share == 0)(lambda: fill_own(width, octants, own_copies, *parts[:3], own_ref))
 
 
 def edge_kernel(side, sent_ref, own_ref, *refs):
@@ -200,53 +252,70 @@
         edge_ref[:, at : at + LANES] = block + own if at == near else block
 
 
-def turn_kernel(width, other, side, edge_ref, own_ref, *refs):
-    half = lax.rem(lax.axis_index("off") + other, 2)
-    shifted = refs[-1]
+def turn(width, half, side, edge_ref, own_ref, shifted):
     blocks = [edge_ref[:, :LANES], edge_ref[:, LANES:]]
     if side == 0:
         blocks.append(own_ref[half, :, LANES : 2 * LANES])
     stacks = [jnp.concatenate(halves(block), axis=0) for block in blocks]
     lane = lax.broadcasted_iota(i32, stacks[0].shape, 1)
-    for turn in range(LANES // width):
-        tiles = [pltpu.roll(stack, LANES - width * turn, 1) for stack in stacks] if turn else stacks
-        kept = lane < LANES - width * turn
-        row = turn * WINDOW
+    for by in range(LANES // width):
+        tiles = [pltpu.roll(stack, LANES - width * by, 1) for stack in stacks] if by else stacks
+        kept = lane < LANES - width * by
+        row = by * WINDOW
         if side == 0:
-            shifted[row] = jnp.where(kept, tiles[0], tiles[1]) if turn else tiles[0]
-            shifted[row + 1] = jnp.where(kept, tiles[1], tiles[2]) if turn else tiles[1]
+            shifted[row] = jnp.where(kept, tiles[0], tiles[1]) if by else tiles[0]
+            shifted[row + 1] = jnp.where(kept, tiles[1], tiles[2]) if by else tiles[1]
             shifted[row + 2] = tiles[2]
         else:
-            if turn:
+            if by:
                 shifted[row + 2] = jnp.where(kept, shifted[row + 2], tiles[0])
-            shifted[row + 3] = jnp.where(kept, tiles[0], tiles[1]) if turn else tiles[0]
-            if not turn:
+            shifted[row + 3] = jnp.where(kept, tiles[0], tiles[1]) if by else tiles[0]
+            if not by:
                 shifted[row + 4] = tiles[1]
-
-
-def multiply_kernel(width, other, split_ref, mask_ref, place_ref, shifted, *refs):
+        yield
+
+
+def turn_kernel(width, other, side, edge_ref, own_ref, *refs):
     half = lax.rem(lax.axis_index("off") + other, 2)
-    points = split_ref.shape[2]
-    span = TGT * width
-    if other:
-        sum_ref, *out_refs = refs
-    else:
-        (sum_ref,) = refs
-    total = sum_ref[...] if other else jnp.zeros((points, span), f32)
-    none = jnp.zeros((TAIL, span), bf16)
-    for at in range(mask_ref.shape[0]):
+    for _ in turn(width, half, side, edge_ref, own_ref, refs[-1]):
+        pass
+
+
+def products(half, begin, end, split_ref, mask_ref, place_ref, shifted, total, beside=()):
+    beside = iter(beside)
+    none = jnp.zeros((TAIL, total.shape[1]), bf16)
+    for at in range(begin, end):
         place = place_ref[at]
         here = mask_ref[at : at + 1, :].astype(bf16)
         both = jnp.concatenate([shifted[place], shifted[place + 1]], axis=1) * here
         high, high_tail, low, low_tail = both[:BODY], both[BODY:HALF], both[HALF : HALF + BODY], both[HALF + BODY :]
         depth = [high, high, low, high_tail, high_tail, low_tail, none]
         total += jnp.dot(split_ref[at, half], jnp.concatenate(depth, axis=0), preferred_element_type=f32)
-    if not other:
-        sum_ref[...] = total
-        return
+        if (at - begin) % 2:
+            next(beside, None)
+    for _ in beside:
+        pass
+    return total
+
+
+def first_kernel(begin, end, split_ref, mask_ref, place_ref, shifted, sum_ref):
+    half = lax.rem(lax.axis_index("off"), 2)
+    total = jnp.zeros(sum_ref.shape, f32)
+    sum_ref[...] = products(half, begin, end, split_ref, mask_ref, place_ref, shifted, total)
+
+
+def beside_kernel(width, begin, end, split_ref, mask_ref, place_ref, shifted, before, edge_ref, own_ref, sum_ref, turned):
+    half = lax.rem(lax.axis_index("off"), 2)
+    turns = turn(width, 1 - half, 0, edge_ref, own_ref, turned)
+    sum_ref[...] = products(half, begin, end, split_ref, mask_ref, place_ref, shifted, before[...], turns)
+
+
+def second_kernel(split_ref, mask_ref, place_ref, shifted, before, *out_refs):
+    me = lax.axis_index("off")
+    half = lax.rem(me + 1, 2)
+    total = products(half, 0, mask_ref.shape[0], split_ref, mask_ref, place_ref, shifted, before[...])
     shares = len(out_refs)
-    lanes = span // shares
-    me = lax.axis_index("off")
+    lanes = total.shape[1] // shares
     for step, out_ref in enumerate(out_refs):
         piece = total[:, :lanes]
         for share in range(1, shares):
@@ -298,41 +367,54 @@
         return lambda *operands: run(*map(pltpu.with_memory_space_constraint, operands, places))
 
     half_shape = pltpu.VMEM((HALF, span), f32)
-    to_right, to_left, table = call(
+    slots = slot_octant.shape[0]
+    to_right, to_left = call(
         functools.partial(table_kernel, width, octants),
         "table",
-        [half_shape, half_shape, pltpu.VMEM((TGT + 2 * SPILL, 2 * HALF * width), f32)],
+        [half_shape, half_shape],
         [hbm] * 2,
-        [pltpu.SMEM(slot_octant.shape, i32), pltpu.VMEM(contrib.shape, f32), pltpu.SemaphoreType.DMA((2,))],
+        [
+            pltpu.SMEM((slots,), i32),
+            pltpu.VMEM((slots, HALF * width), f32),
+            pltpu.VMEM((TGT + 2 * SPILL, HALF * width), f32),
+            pltpu.SemaphoreType.DMA((2 + slots // ROWS,)),
+        ],
     )(slot_octant, contrib)
 
     forward = [(i, (i + 1) % count) for i in range(count)]
     backward = [(target, source) for source, target in forward]
     low = lax.ppermute(to_right, "dom", forward)
 
-    step = classes * 7 // 40
+    step = classes * 6 // 40
     bounds = [step * at for at in range(STEPS + 1)]
     bounds += [(bounds[-1] + classes) // 2, classes]
     split_shape = pltpu.VMEM((classes, 2, points, 2 * LANES), bf16)
     own_shape = pltpu.VMEM((2, HALF, 3 * LANES), f32)
     blocks = pltpu.VMEM(translation.shape, f32)
+    own_parts = [
+        pltpu.SMEM((slots,), i32),
+        pltpu.VMEM(contrib.shape, f32),
+        pltpu.VMEM((TGT + 2 * SPILL, contrib.shape[1]), f32),
+        pltpu.SemaphoreType.DMA((2,)),
+    ]
     split, own, to_left = call(
-        functools.partial(early_kernel, width, bounds),
+        functools.partial(early_kernel, width, octants, bounds),
         "early",
         [split_shape, own_shape, half_shape],
-        [hbm, vmem, vmem],
-        [blocks, pltpu.SemaphoreType.DMA((STEPS,))],
-    )(translation, table, to_left)
+        [hbm] * 3 + [vmem],
+        [blocks, pltpu.SemaphoreType.DMA((STEPS,))] + own_parts,
+        input_output_aliases={3: 2},
+    )(slot_octant, contrib, translation, to_left)
     high = lax.ppermute(to_left, "dom", backward)
     tables = [pltpu.VMEM(vlist_src.shape, i32), pltpu.VMEM(vlist_class.shape, i32)]
     split, own, *facts = call(
         functools.partial(late_kernel, width, octants, bounds),
         "late",
         [split_shape, own_shape, pltpu.VMEM((classes, span), f32), pltpu.SMEM((classes,), i32)],
-        [hbm] * 3 + [vmem] * 3,
-        tables + [blocks, pltpu.SemaphoreType.DMA((len(bounds) - 1,)), pltpu.SemaphoreType.DMA((2,))],
-        input_output_aliases={4: 0, 5: 1},
-    )(vlist_src, vlist_class, translation, table, split, own)
+        [hbm] * 5 + [vmem] * 2,
+        tables + [blocks, pltpu.SemaphoreType.DMA((len(bounds) - 1,)), pltpu.SemaphoreType.DMA((2,))] + own_parts,
+        input_output_aliases={5: 0, 6: 1},
+    )(vlist_src, vlist_class, slot_octant, contrib, translation, split, own)
     facts.insert(0, split)
 
     twins = [(i, i ^ 1) for i in range(shares)]
@@ -356,15 +438,19 @@
     right = edge(1, high, window, vmem)
     right_other = lax.ppermute(right, "off", twins)
     window = turned(0, 1, right, window)
-    total = call(
-        functools.partial(multiply_kernel, width, 0), "first", pltpu.VMEM((points, span), f32), [vmem, vmem, smem, vmem]
-    )(*facts, window)
-    window = turned(1, 1, right_other, turned(1, 0, left_other))
+    sum_shape = pltpu.VMEM((points, span), f32)
+    middle = classes // 2
+    tables = [vmem, vmem, smem]
+    total = call(functools.partial(first_kernel, 0, middle), "first", sum_shape, tables + [vmem])(*facts, window)
+    total, window = call(
+        functools.partial(beside_kernel, width, middle, classes),
+        "first_beside_turns",
+        [sum_shape, turned_shape],
+        tables + [vmem] * 4,
+    )(*facts, window, total, left_other, own)
+    window = turned(1, 1, right_other, window)
     shares_out = call(
-        functools.partial(multiply_kernel, width, 1),
-        "second",
-        [pltpu.VMEM((points, span // shares), f32)] * shares,
-        [vmem, vmem, smem, vmem, vmem],
+        second_kernel, "second", [pltpu.VMEM((points, span // shares), f32)] * shares, tables + [vmem] * 2
     )(*facts, window, total)
 
     pieces = [shares_out[0]]

time: 17 us -> 16.8 us (0.988)
    ppermute x1, waiting for transfers between devices: 0.18 us -> 0.01 us  [local(): low = lax.ppermute(to_right, 'dom', forward)]
  transfers between devices with their start and end apart: 5 -> 5, of which waited for: 3 -> 2; matrix products, arithmetic and copies ran while one was open for 0% -> 0% of each run, Pallas kernels for 40% -> 42%
where the time goes in v2:
time: 16.8 us; the launch traced here: 16.6 us
  Pallas kernels  10.2 us (61%)
  starting transfers between devices  5.01 us (30%)
  waiting for transfers between devices  1.29 us (8%)
    pallas_call x12, Pallas kernels, call(): run(*map(pltpu.with_memory_space_constraint, operands, places))  10.2 us
    ppermute x1, starting transfers between devices, local(): low = lax.ppermute(to_right, 'dom', forward)  2.99 us
    ppermute x1, starting transfers between devices, local(): high = lax.ppermute(to_left, 'dom', backward)  1.31 us
    ppermute x1, waiting for transfers between devices, local(): pieces.append(lax.ppermute(shares_out[step], 'off', pairs))  0.92 us
    ppermute x1, starting transfers between devices, local(): pieces.append(lax.ppermute(shares_out[step], 'off', pairs))  0.42 us
    ppermute x1, waiting for transfers between devices, local(): high = lax.ppermute(to_left, 'dom', backward)  0.36 us
  transfers between devices with their start and end apart: 5, of which 2 were waited for; matrix products, arithmetic and copies ran while one was open for 0% of the time, Pallas kernels for 42%

profile of v2, /device:TPU:0, one launch (start us, length us, event | category | flops | bytes accessed | tf_op | source)
XLA Modules:
  0.0 16.6 jit_solution(11938984425306685715)
XLA Ops:
  0.0 1.1 %table.1 = (f32[80,256]{1,0:T(8,128)S(1)}, f32[80,256]{1,0:T(8,128)S(1)}) custom-call(s32[24]{0:T(128)} %slot_hbm.5, f32[24,2432]{1,0:T(8,128)} %contrib_hbm.5), custom_call_target="tpu_custom_call" | custom-call | tf_op jit(solution)/shard_map/table/pallas_call | solution.py:367
  1.1 3.0 %collective-permute-start.1 = (f32[80,256]{1,0:T(8,128)S(1)}, f32[80,256]{1,0:T(8,128)S(1)}, u32[]{:S(2)}, u32[]{:S(2)}) collective-permute-start(f32[80,256]{1,0:T(8,128)S(1)} %get-tuple-element.26), channel_id=1, source_target_pairs={{0,2},{2,4},{4,6},{6,8},{8,10},{10,12},{12,14},{14,16},{16,18},{18... | collective-permute-start | bytes 245768 | tf_op jit(solution)/shard_map/ppermute | solution.py:386
  4.1 2.8 %early.1 = (bf16[40,2,152,256]{3,2,1,0:T(8,128)(2,1)S(1)}, f32[2,80,384]{2,1,0:T(8,128)S(1)}, f32[80,256]{1,0:T(8,128)S(1)}) custom-call(s32[24]{0:T(128)} %slot_hbm.5, f32[24,2432]{1,0:T(8,128)} %contrib_hbm.5, f32[40,152,152]{2,1,0:T(8,128)} %block_hbm.3, f32[80,256]{1,0:T(8,128)S(1)} %get-tuple-element.18._sent), custom_call_target="tpu_custom_call", output_to_operand_aliasing={{2}: (3, {})} | custom-call | tf_op jit(solution)/shard_map/early/pallas_call | solution.py:367
  6.9 1.3 %collective-permute-start = (f32[80,256]{1,0:T(8,128)S(1)}, f32[80,256]{1,0:T(8,128)S(1)}, u32[]{:S(2)}, u32[]{:S(2)}) collective-permute-start(f32[80,256]{1,0:T(8,128)S(1)} %get-tuple-element.24), channel_id=1, source_target_pairs={{2,0},{4,2},{6,4},{8,6},{10,8},{12,10},{14,12},{16,14},{18,16},{20... | collective-permute-start | bytes 245768 | tf_op jit(solution)/shard_map/ppermute | solution.py:408
  8.2 2.4 %late.1 = (bf16[40,2,152,256]{3,2,1,0:T(8,128)(2,1)S(1)}, f32[2,80,384]{2,1,0:T(8,128)S(1)}, f32[40,256]{1,0:T(8,128)S(1)}, s32[40]{0:T(128)S(4)}) custom-call(s32[16,40]{1,0:T(8,128)} %src_hbm.1, s32[16,40]{1,0:T(8,128)} %class_hbm.1, s32[24]{0:T(128)} %slot_hbm.5, f32[24,2432]{1,0:T(8,128)} %contrib_hbm.5, ...), custom_call_target="tpu_custom_call", output_to_operand_aliasing={{0}: (5, {}), {1}: (6, {})} | custom-call | tf_op jit(solution)/shard_map/late/pallas_call | solution.py:367
  10.6 0.0 collective-permute-done.1.sent_ref
  10.7 0.1 collective-permute-start.3
  10.8 0.3 %left_turns.1.refs_0_ = bf16[40,160,128]{2,1,0:T(8,128)(2,1)S(1)} custom-call(f32[80,256]{1,0:T(8,128)S(1)} %edge.2.edge_ref, f32[2,80,384]{2,1,0:T(8,128)S(1)} %get-tuple-element.25.own_ref), custom_call_target="tpu_custom_call" | custom-call | tf_op jit(solution)/shard_map/left_turns/pallas_call | solution.py:367
  11.1 0.4 %collective-permute-done.sent_ref = f32[80,256]{1,0:T(8,128)S(1)} collective-permute-done((f32[80,256]{1,0:T(8,128)S(1)}, f32[80,256]{1,0:T(8,128)S(1)}, u32[]{:S(2)}, u32[]{:S(2)}) %collective-permute-start) | collective-permute-done | bytes 81952 | tf_op jit(solution)/shard_map/ppermute | solution.py:408
  11.4 0.2 %collective-permute-start.2 = (f32[80,256]{1,0:T(8,128)S(1)}, f32[80,256]{1,0:T(8,128)S(1)}, u32[]{:S(2)}, u32[]{:S(2)}) collective-permute-start(f32[80,256]{1,0:T(8,128)S(1)} %edge.3.edge_ref), channel_id=1, source_target_pairs={{0,1},{1,0},{2,3},{3,2},{4,5},{5,4},{6,7},{7,6},{8,9},{9,8},{10,11... | collective-permute-start | bytes 245768 | tf_op jit(solution)/shard_map/ppermute | solution.py:439
  11.6 0.2 %right_turns.2.shifted = bf16[40,160,128]{2,1,0:T(8,128)(2,1)S(1)} custom-call(f32[80,256]{1,0:T(8,128)S(1)} %edge.3.edge_ref, f32[2,80,384]{2,1,0:T(8,128)S(1)} %get-tuple-element.25.own_ref, bf16[40,160,128]{2,1,0:T(8,128)(2,1)S(1)} %left_turns.1.refs_0_), custom_call_target="tpu_custom_call", output_to_operand_aliasing={{}: (2, {})} | custom-call | tf_op jit(solution)/shard_map/right_turns/pallas_call | solution.py:367
  11.9 0.6 %first.1.before = f32[152,256]{1,0:T(8,128)S(1)} custom-call(bf16[40,2,152,256]{3,2,1,0:T(8,128)(2,1)S(1)} %get-tuple-element.21.split_ref, f32[40,256]{1,0:T(8,128)S(1)} %get-tuple-element.22.mask_ref, s32[40]{0:T(128)S(4)} %get-tuple-element.23.refs_0_.place_ref, bf16[40,160,128]{2,1,0:T(8,128)(2,1)S(1)} %right_turns.2.shifted), custom_call_target="tpu_custom_call" | custom-call | tf_op jit(solution)/shard_map/first/pallas_call | solution.py:367
  12.5 0.0 collective-permute-done.3.edge_ref
  12.5 0.6 %first_beside_turns.1 = (f32[152,256]{1,0:T(8,128)S(1)}, bf16[40,160,128]{2,1,0:T(8,128)(2,1)S(1)}) custom-call(bf16[40,2,152,256]{3,2,1,0:T(8,128)(2,1)S(1)} %get-tuple-element.21.split_ref, f32[40,256]{1,0:T(8,128)S(1)} %get-tuple-element.22.mask_ref, s32[40]{0:T(128)S(4)} %get-tuple-element.23.refs_0_.place_ref, ...), custom_call_target="tpu_custom_call" | custom-call | tf_op jit(solution)/shard_map/first_beside_turns/pallas_call | solution.py:367
  13.1 0.0 collective-permute-done.2.edge_ref
  13.2 0.2 %right_turns.3.shifted = bf16[40,160,128]{2,1,0:T(8,128)(2,1)S(1)} custom-call(f32[80,256]{1,0:T(8,128)S(1)} %collective-permute-done.2.edge_ref, f32[2,80,384]{2,1,0:T(8,128)S(1)} %get-tuple-element.25.own_ref, bf16[40,160,128]{2,1,0:T(8,128)(2,1)S(1)} %get-tuple-element.27.refs_0_), custom_call_target="tpu_custom_call", output_to_operand_aliasing={{}: (2, {})} | custom-call | tf_op jit(solution)/shard_map/right_turns/pallas_call | solution.py:367
  13.4 1.1 %second.1 = (f32[152,128]{1,0:T(8,128)S(1)}, f32[152,128]{1,0:T(8,128)S(1)}) custom-call(bf16[40,2,152,256]{3,2,1,0:T(8,128)(2,1)S(1)} %get-tuple-element.21.split_ref, f32[40,256]{1,0:T(8,128)S(1)} %get-tuple-element.22.mask_ref, s32[40]{0:T(128)S(4)} %get-tuple-element.23.refs_0_.place_ref, bf16[40,160,128]{2,1,0:T(8,128)(2,1)S(1)} %right_turns.3.shifted, ...), custom_call_target="tpu_custom_call" | custom-call | tf_op jit(solution)/shard_map/second/pallas_call | solution.py:367
  14.5 0.4 %collective-permute-start.4 = (f32[152,128]{1,0:T(8,128)S(1)}, f32[152,128]{1,0:T(8,128)S(1)}, u32[]{:S(2)}, u32[]{:S(2)}) collective-permute-start(f32[152,128]{1,0:T(8,128)S(1)} %get-tuple-element.30), channel_id=1, source_target_pairs={{0,1},{1,0},{2,3},{3,2},{4,5},{5,4},{6,7},{7,6},{8,9},{9,8},{10,11... | collective-permute-start | bytes 233480 | tf_op jit(solution)/shard_map/ppermute | solution.py:459
  14.9 0.9 %collective-permute-done.4.refs_1_ = f32[152,128]{1,0:T(8,128)S(1)} collective-permute-done((f32[152,128]{1,0:T(8,128)S(1)}, f32[152,128]{1,0:T(8,128)S(1)}, u32[]{:S(2)}, u32[]{:S(2)}) %collective-permute-start.4) | collective-permute-done | bytes 77856 | tf_op jit(solution)/shard_map/ppermute | solution.py:459
  15.8 0.8 %finish.1 = f32[8,2432]{1,0:T(8,128)} custom-call(f32[152,128]{1,0:T(8,128)S(1)} %get-tuple-element.29.refs_0_, f32[152,128]{1,0:T(8,128)S(1)} %collective-permute-done.4.refs_1_), custom_call_target="tpu_custom_call" | custom-call | tf_op jit(solution)/shard_map/finish/pallas_call | solution.py:367
  (2 shorter events, 0.0 us)
Async XLA Ops:
  1.1 9.6 %collective-permute-start.1 = (f32[80,256]{1,0:T(8,128)S(1)}, f32[80,256]{1,0:T(8,128)S(1)}, u32[]{:S(2)}, u32[]{:S(2)}) collective-permute-start(f32[80,256]{1,0:T(8,128)S(1)} %get-tuple-element.26), channel_id=1, source_target_pairs={{0,2},{2,4},{4,6},{6,8},{8,10},{10,12},{12,14},{14,16},{16,18},{18... | collective-permute-start | bytes 245768 | tf_op jit(solution)/shard_map/ppermute | solution.py:386
  6.9 4.5 %collective-permute-start = (f32[80,256]{1,0:T(8,128)S(1)}, f32[80,256]{1,0:T(8,128)S(1)}, u32[]{:S(2)}, u32[]{:S(2)}) collective-permute-start(f32[80,256]{1,0:T(8,128)S(1)} %get-tuple-element.24), channel_id=1, source_target_pairs={{2,0},{4,2},{6,4},{8,6},{10,8},{12,10},{14,12},{16,14},{18,16},{20... | collective-permute-start | bytes 245768 | tf_op jit(solution)/shard_map/ppermute | solution.py:408
  10.7 1.8 %collective-permute-start.3 = (f32[80,256]{1,0:T(8,128)S(1)}, f32[80,256]{1,0:T(8,128)S(1)}, u32[]{:S(2)}, u32[]{:S(2)}) collective-permute-start(f32[80,256]{1,0:T(8,128)S(1)} %edge.2.edge_ref), channel_id=1, source_target_pairs={{0,1},{1,0},{2,3},{3,2},{4,5},{5,4},{6,7},{7,6},{8,9},{9,8},{10,11... | collective-permute-start | bytes 245768 | tf_op jit(solution)/shard_map/ppermute | solution.py:436
  11.4 1.7 %collective-permute-start.2 = (f32[80,256]{1,0:T(8,128)S(1)}, f32[80,256]{1,0:T(8,128)S(1)}, u32[]{:S(2)}, u32[]{:S(2)}) collective-permute-start(f32[80,256]{1,0:T(8,128)S(1)} %edge.3.edge_ref), channel_id=1, source_target_pairs={{0,1},{1,0},{2,3},{3,2},{4,5},{5,4},{6,7},{7,6},{8,9},{9,8},{10,11... | collective-permute-start | bytes 245768 | tf_op jit(solution)/shard_map/ppermute | solution.py:439
  14.5 1.3 %collective-permute-start.4 = (f32[152,128]{1,0:T(8,128)S(1)}, f32[152,128]{1,0:T(8,128)S(1)}, u32[]{:S(2)}, u32[]{:S(2)}) collective-permute-start(f32[152,128]{1,0:T(8,128)S(1)} %get-tuple-element.30), channel_id=1, source_target_pairs={{0,1},{1,0},{2,3},{3,2},{4,5},{5,4},{6,7},{7,6},{8,9},{9,8},{10,11... | collective-permute-start | bytes 233480 | tf_op jit(solution)/shard_map/ppermute | solution.py:459

commit v3 on v2

--- a/solution.py
+++ b/solution.py
@@ -180,17 +180,28 @@
     return jnp.clip(STEPS - lax.axis_index("dom") * 3 // 2, 0, STEPS)
 
 
+def own_kernel(width, octants, slot_hbm, contrib_hbm, _sent, own_ref, _passed, *parts):
+    @pl.when(lax.axis_index("dom") == 0)
+    def _():
+        own_copies = fetch_own(slot_hbm, contrib_hbm, *parts)
+        for copy in own_copies:
+            copy.start()
+        fill_own(width, octants, own_copies, *parts[:3], own_ref)
+
+
 def early_kernel(
-    width, octants, bounds, slot_hbm, contrib_hbm, block_hbm, _sent, split_ref, own_ref, _copied, block_ref, sems, *parts
+    width, octants, bounds, slot_hbm, contrib_hbm, block_hbm, _own, _sent, split_ref, own_ref, _passed,
+    block_ref, sems, *parts
 ):
     share = early_share()
     copies = [fetch(block_hbm, block_ref, sems.at[step], *bounds[step : step + 2]) for step in range(STEPS)]
     own_copies = fetch_own(slot_hbm, contrib_hbm, *parts)
+    fills = (share > 0) & (lax.axis_index("dom") > 0)
 
     @pl.when(share > 0)
     def _():
         for copy in own_copies:
-            copy.start()
+            pl.when(fills)(copy.start)
         for step in range(STEPS):
             pl.when(step < share)(copies[step].start)
         places = tail_places()
@@ -201,7 +212,7 @@
                 copies[step].wait()
                 split_blocks(places, bounds[step], bounds[step + 1], block_ref, split_ref)
 
-        fill_own(width, octants, own_copies, *parts[:3], own_ref)
+    pl.when(fills)(lambda: fill_own(width, octants, own_copies, *parts[:3], own_ref))
 
 
 def late_kernel(
@@ -242,18 +253,19 @@
     pl.when(share == 0)(lambda: fill_own(width, octants, own_copies, *parts[:3], own_ref))
 
 
-def edge_kernel(side, sent_ref, own_ref, *refs):
+def edge_kernel(sides, own_ref, *refs):
     half = lax.rem(lax.axis_index("off"), 2)
-    near = LANES * (1 - side)
-    edge_ref = refs[-1]
-    own = own_ref[half, :, 2 * LANES * side : 2 * LANES * side + LANES]
-    for at in range(0, 2 * LANES, LANES):
-        block = sent_ref[:, at : at + LANES]
-        edge_ref[:, at : at + LANES] = block + own if at == near else block
+    for at, side in enumerate(sides):
+        own = own_ref[half, :, 2 * LANES * side : 2 * LANES * side + LANES]
+        for block in range(2):
+            lanes = slice(LANES * (2 * at + block), LANES * (2 * at + block + 1))
+            sent = refs[at][:, LANES * block : LANES * (block + 1)]
+            refs[-1][:, lanes] = sent + own if block == 1 - side else sent
 
 
 def turn(width, half, side, edge_ref, own_ref, shifted):
-    blocks = [edge_ref[:, :LANES], edge_ref[:, LANES:]]
+    begin = edge_ref.shape[1] - 2 * LANES if side else 0
+    blocks = [edge_ref[:, begin : begin + LANES], edge_ref[:, begin + LANES : begin + 2 * LANES]]
     if side == 0:
         blocks.append(own_ref[half, :, LANES : 2 * LANES])
     stacks = [jnp.concatenate(halves(block), axis=0) for block in blocks]
@@ -304,12 +316,6 @@
     sum_ref[...] = products(half, begin, end, split_ref, mask_ref, place_ref, shifted, total)
 
 
-def beside_kernel(width, begin, end, split_ref, mask_ref, place_ref, shifted, before, edge_ref, own_ref, sum_ref, turned):
-    half = lax.rem(lax.axis_index("off"), 2)
-    turns = turn(width, 1 - half, 0, edge_ref, own_ref, turned)
-    sum_ref[...] = products(half, begin, end, split_ref, mask_ref, place_ref, shifted, before[...], turns)
-
-
 def second_kernel(split_ref, mask_ref, place_ref, shifted, before, *out_refs):
     me = lax.axis_index("off")
     half = lax.rem(me + 1, 2)
@@ -383,28 +389,36 @@
 
     forward = [(i, (i + 1) % count) for i in range(count)]
     backward = [(target, source) for source, target in forward]
-    low = lax.ppermute(to_right, "dom", forward)
-
-    step = classes * 6 // 40
-    bounds = [step * at for at in range(STEPS + 1)]
-    bounds += [(bounds[-1] + classes) // 2, classes]
-    split_shape = pltpu.VMEM((classes, 2, points, 2 * LANES), bf16)
-    own_shape = pltpu.VMEM((2, HALF, 3 * LANES), f32)
-    blocks = pltpu.VMEM(translation.shape, f32)
     own_parts = [
         pltpu.SMEM((slots,), i32),
         pltpu.VMEM(contrib.shape, f32),
         pltpu.VMEM((TGT + 2 * SPILL, contrib.shape[1]), f32),
         pltpu.SemaphoreType.DMA((2,)),
     ]
+    own_shape = pltpu.VMEM((2, HALF, 3 * LANES), f32)
+    own, to_right = call(
+        functools.partial(own_kernel, width, octants),
+        "own",
+        [own_shape, half_shape],
+        [hbm] * 2 + [vmem],
+        own_parts,
+        input_output_aliases={2: 1},
+    )(slot_octant, contrib, to_right)
+    low = lax.ppermute(to_right, "dom", forward)
+
+    step = classes * 5 // 40
+    bounds = [step * at for at in range(STEPS + 1)]
+    bounds += [(bounds[-1] + classes) // 2, classes]
+    split_shape = pltpu.VMEM((classes, 2, points, 2 * LANES), bf16)
+    blocks = pltpu.VMEM(translation.shape, f32)
     split, own, to_left = call(
         functools.partial(early_kernel, width, octants, bounds),
         "early",
         [split_shape, own_shape, half_shape],
-        [hbm] * 3 + [vmem],
+        [hbm] * 3 + [vmem] * 2,
         [blocks, pltpu.SemaphoreType.DMA((STEPS,))] + own_parts,
-        input_output_aliases={3: 2},
-    )(slot_octant, contrib, translation, to_left)
+        input_output_aliases={3: 1, 4: 2},
+    )(slot_octant, contrib, translation, own, to_left)
     high = lax.ppermute(to_left, "dom", backward)
     tables = [pltpu.VMEM(vlist_src.shape, i32), pltpu.VMEM(vlist_class.shape, i32)]
     split, own, *facts = call(
@@ -429,26 +443,17 @@
             **({"input_output_aliases": {2: 0}} if before else {}),
         )(edge, own, *before)
 
-    def edge(side, sent, after, spec):
-        return call(functools.partial(edge_kernel, side), "edge", half_shape, [vmem] * 2 + [spec])(sent, own, after)
-
-    left = edge(0, low, facts[2], smem)
-    left_other = lax.ppermute(left, "off", twins)
+    left = call(functools.partial(edge_kernel, [0]), "edge", half_shape, [vmem, vmem, smem])(own, low, facts[2])
     window = turned(0, 0, left)
-    right = edge(1, high, window, vmem)
-    right_other = lax.ppermute(right, "off", twins)
-    window = turned(0, 1, right, window)
+    edges = call(
+        functools.partial(edge_kernel, [0, 1]), "edges", pltpu.VMEM((HALF, 4 * LANES), f32), [vmem] * 4
+    )(own, low, high, window)
+    edges_other = lax.ppermute(edges, "off", twins)
+    window = turned(0, 1, edges, window)
     sum_shape = pltpu.VMEM((points, span), f32)
-    middle = classes // 2
     tables = [vmem, vmem, smem]
-    total = call(functools.partial(first_kernel, 0, middle), "first", sum_shape, tables + [vmem])(*facts, window)
-    total, window = call(
-        functools.partial(beside_kernel, width, middle, classes),
-        "first_beside_turns",
-        [sum_shape, turned_shape],
-        tables + [vmem] * 4,
-    )(*facts, window, total, left_other, own)
-    window = turned(1, 1, right_other, window)
+    total = call(functools.partial(first_kernel, 0, classes), "first", sum_shape, tables + [vmem])(*facts, window)
+    window = turned(1, 1, edges_other, turned(1, 0, edges_other))
     shares_out = call(
         second_kernel, "second", [pltpu.VMEM((points, span // shares), f32)] * shares, tables + [vmem] * 2
     )(*facts, window, total)

time: 16.8 us -> 16.8 us (level)
  Pallas kernels: 10.2 us -> 11.3 us
  starting transfers between devices: 5.01 us -> 4.09 us
  waiting for transfers between devices: 1.29 us -> 1.06 us
    ppermute x1, starting transfers between devices: 2.99 us -> 1.74 us  [local(): low = lax.ppermute(to_right, 'dom', forward)]
    pallas_call x12 -> x13, Pallas kernels: 10.2 us -> 11.3 us  [call(): run(*map(pltpu.with_memory_space_constraint, operands, places))]
    ppermute x1, starting transfers between devices: 1.31 us -> 1.81 us  [local(): high = lax.ppermute(to_left, 'dom', backward)]
    ppermute x1, waiting for transfers between devices: 0.36 us -> 0.01 us  [local(): high = lax.ppermute(to_left, 'dom', backward)]
    ppermute x2 -> x1, starting transfers between devices: 0.29 us -> 0.07 us  [local(): edges_other = lax.ppermute(edges, 'off', twins)]
  transfers between devices with their start and end apart: 5 -> 4, of which waited for: 2 -> 2; matrix products, arithmetic and copies ran while one was open for 0% -> 0% of each run, Pallas kernels for 42% -> 39%
where the time goes in v3:
time: 16.8 us; the launch traced here: 16.5 us
  Pallas kernels  11.3 us (67%)
  starting transfers between devices  4.09 us (24%)
  waiting for transfers between devices  1.06 us (6%)
    pallas_call x13, Pallas kernels, call(): run(*map(pltpu.with_memory_space_constraint, operands, places))  11.3 us
    ppermute x1, starting transfers between devices, local(): high = lax.ppermute(to_left, 'dom', backward)  1.81 us
    ppermute x1, starting transfers between devices, local(): low = lax.ppermute(to_right, 'dom', forward)  1.74 us
    ppermute x1, waiting for transfers between devices, local(): pieces.append(lax.ppermute(shares_out[step], 'off', pairs))  0.92 us
    ppermute x1, starting transfers between devices, local(): pieces.append(lax.ppermute(shares_out[step], 'off', pairs))  0.47 us
  transfers between devices with their start and end apart: 4, of which 2 were waited for; matrix products, arithmetic and copies ran while one was open for 0% of the time, Pallas kernels for 39%

profile of v3, /device:TPU:0, one launch (start us, length us, event | category | flops | bytes accessed | tf_op | source)
XLA Modules:
  0.0 16.5 jit_solution(1178565952112925373)
XLA Ops:
  0.0 1.1 %table.1 = (f32[80,256]{1,0:T(8,128)S(1)}, f32[80,256]{1,0:T(8,128)S(1)}) custom-call(s32[24]{0:T(128)} %slot_hbm.7, f32[24,2432]{1,0:T(8,128)} %contrib_hbm.7), custom_call_target="tpu_custom_call" | custom-call | tf_op jit(solution)/shard_map/table/pallas_call | solution.py:373
  1.1 1.3 %own.1 = (f32[2,80,384]{2,1,0:T(8,128)S(1)}, f32[80,256]{1,0:T(8,128)S(1)}) custom-call(s32[24]{0:T(128)} %slot_hbm.7, f32[24,2432]{1,0:T(8,128)} %contrib_hbm.7, f32[80,256]{1,0:T(8,128)S(1)} %get-tuple-element.18._sent), custom_call_target="tpu_custom_call", output_to_operand_aliasing={{1}: (2, {})} | custom-call | tf_op jit(solution)/shard_map/own/pallas_call | solution.py:373
  2.4 1.7 %collective-permute-start = (f32[80,256]{1,0:T(8,128)S(1)}, f32[80,256]{1,0:T(8,128)S(1)}, u32[]{:S(2)}, u32[]{:S(2)}) collective-permute-start(f32[80,256]{1,0:T(8,128)S(1)} %get-tuple-element.27), channel_id=1, source_target_pairs={{0,2},{2,4},{4,6},{6,8},{8,10},{10,12},{12,14},{14,16},{16,18},{18... | collective-permute-start | bytes 245768 | tf_op jit(solution)/shard_map/ppermute | solution.py:407
  4.1 2.3 %early.1 = (bf16[40,2,152,256]{3,2,1,0:T(8,128)(2,1)S(1)}, f32[2,80,384]{2,1,0:T(8,128)S(1)}, f32[80,256]{1,0:T(8,128)S(1)}) custom-call(s32[24]{0:T(128)} %slot_hbm.7, f32[24,2432]{1,0:T(8,128)} %contrib_hbm.7, f32[40,152,152]{2,1,0:T(8,128)} %block_hbm.3, f32[2,80,384]{2,1,0:T(8,128)S(1)} %get-tuple-element.19._own, ...), custom_call_target="tpu_custom_call", output_to_operand_aliasing={{1}: (3, {}), {2}: (4, {})} | custom-call | tf_op jit(solution)/shard_map/early/pallas_call | solution.py:373
  6.5 1.8 %collective-permute-start.1 = (f32[80,256]{1,0:T(8,128)S(1)}, f32[80,256]{1,0:T(8,128)S(1)}, u32[]{:S(2)}, u32[]{:S(2)}) collective-permute-start(f32[80,256]{1,0:T(8,128)S(1)} %get-tuple-element.28), channel_id=1, source_target_pairs={{2,0},{4,2},{6,4},{8,6},{10,8},{12,10},{14,12},{16,14},{18,16},{20... | collective-permute-start | bytes 245768 | tf_op jit(solution)/shard_map/ppermute | solution.py:422
  8.3 2.6 %late.1 = (bf16[40,2,152,256]{3,2,1,0:T(8,128)(2,1)S(1)}, f32[2,80,384]{2,1,0:T(8,128)S(1)}, f32[40,256]{1,0:T(8,128)S(1)}, s32[40]{0:T(128)S(4)}) custom-call(s32[16,40]{1,0:T(8,128)} %src_hbm.1, s32[16,40]{1,0:T(8,128)} %class_hbm.1, s32[24]{0:T(128)} %slot_hbm.7, f32[24,2432]{1,0:T(8,128)} %contrib_hbm.7, ...), custom_call_target="tpu_custom_call", output_to_operand_aliasing={{0}: (5, {}), {1}: (6, {})} | custom-call | tf_op jit(solution)/shard_map/late/pallas_call | solution.py:373
  10.9 0.0 collective-permute-done.refs_0_
  10.9 0.3 %left_turns.2.refs_2_.refs_0_ = bf16[40,160,128]{2,1,0:T(8,128)(2,1)S(1)} custom-call(f32[80,256]{1,0:T(8,128)S(1)} %edge.1.edge_ref, f32[2,80,384]{2,1,0:T(8,128)S(1)} %get-tuple-element.26.own_ref), custom_call_target="tpu_custom_call" | custom-call | tf_op jit(solution)/shard_map/left_turns/pallas_call | solution.py:373
  11.2 0.0 collective-permute-done.1.refs_1_
  11.3 0.1 collective-permute-start.2
  11.4 0.2 %right_turns.3.shifted = bf16[40,160,128]{2,1,0:T(8,128)(2,1)S(1)} custom-call(f32[80,512]{1,0:T(8,128)S(1)} %edges.1.edge_ref, f32[2,80,384]{2,1,0:T(8,128)S(1)} %get-tuple-element.26.own_ref, bf16[40,160,128]{2,1,0:T(8,128)(2,1)S(1)} %left_turns.2.refs_2_.refs_0_), custom_call_target="tpu_custom_call", output_to_operand_aliasing={{}: (2, {})} | custom-call | tf_op jit(solution)/shard_map/right_turns/pallas_call | solution.py:373
  11.6 1.1 %first.1.before = f32[152,256]{1,0:T(8,128)S(1)} custom-call(bf16[40,2,152,256]{3,2,1,0:T(8,128)(2,1)S(1)} %get-tuple-element.23.split_ref, f32[40,256]{1,0:T(8,128)S(1)} %get-tuple-element.24.mask_ref, s32[40]{0:T(128)S(4)} %get-tuple-element.25.refs_1_.place_ref, bf16[40,160,128]{2,1,0:T(8,128)(2,1)S(1)} %right_turns.3.shifted), custom_call_target="tpu_custom_call" | custom-call | tf_op jit(solution)/shard_map/first/pallas_call | solution.py:373
  12.7 0.1 collective-permute-done.2.edge_ref
  12.7 0.3 %left_turns.3.refs_0_ = bf16[40,160,128]{2,1,0:T(8,128)(2,1)S(1)} custom-call(f32[80,512]{1,0:T(8,128)S(1)} %collective-permute-done.2.edge_ref, f32[2,80,384]{2,1,0:T(8,128)S(1)} %get-tuple-element.26.own_ref), custom_call_target="tpu_custom_call" | custom-call | tf_op jit(solution)/shard_map/left_turns/pallas_call | solution.py:373
  13.0 0.2 %right_turns.2.shifted = bf16[40,160,128]{2,1,0:T(8,128)(2,1)S(1)} custom-call(f32[80,512]{1,0:T(8,128)S(1)} %collective-permute-done.2.edge_ref, f32[2,80,384]{2,1,0:T(8,128)S(1)} %get-tuple-element.26.own_ref, bf16[40,160,128]{2,1,0:T(8,128)(2,1)S(1)} %left_turns.3.refs_0_), custom_call_target="tpu_custom_call", output_to_operand_aliasing={{}: (2, {})} | custom-call | tf_op jit(solution)/shard_map/right_turns/pallas_call | solution.py:373
  13.3 1.1 %second.1 = (f32[152,128]{1,0:T(8,128)S(1)}, f32[152,128]{1,0:T(8,128)S(1)}) custom-call(bf16[40,2,152,256]{3,2,1,0:T(8,128)(2,1)S(1)} %get-tuple-element.23.split_ref, f32[40,256]{1,0:T(8,128)S(1)} %get-tuple-element.24.mask_ref, s32[40]{0:T(128)S(4)} %get-tuple-element.25.refs_1_.place_ref, bf16[40,160,128]{2,1,0:T(8,128)(2,1)S(1)} %right_turns.2.shifted, ...), custom_call_target="tpu_custom_call" | custom-call | tf_op jit(solution)/shard_map/second/pallas_call | solution.py:373
  14.3 0.5 %collective-permute-start.3 = (f32[152,128]{1,0:T(8,128)S(1)}, f32[152,128]{1,0:T(8,128)S(1)}, u32[]{:S(2)}, u32[]{:S(2)}) collective-permute-start(f32[152,128]{1,0:T(8,128)S(1)} %get-tuple-element.30), channel_id=1, source_target_pairs={{0,1},{1,0},{2,3},{3,2},{4,5},{5,4},{6,7},{7,6},{8,9},{9,8},{10,11... | collective-permute-start | bytes 233480 | tf_op jit(solution)/shard_map/ppermute | solution.py:464
  14.8 0.9 %collective-permute-done.3.refs_1_ = f32[152,128]{1,0:T(8,128)S(1)} collective-permute-done((f32[152,128]{1,0:T(8,128)S(1)}, f32[152,128]{1,0:T(8,128)S(1)}, u32[]{:S(2)}, u32[]{:S(2)}) %collective-permute-start.3) | collective-permute-done | bytes 77856 | tf_op jit(solution)/shard_map/ppermute | solution.py:464
  15.7 0.8 %finish.1 = f32[8,2432]{1,0:T(8,128)} custom-call(f32[152,128]{1,0:T(8,128)S(1)} %get-tuple-element.29.refs_0_, f32[152,128]{1,0:T(8,128)S(1)} %collective-permute-done.3.refs_1_), custom_call_target="tpu_custom_call" | custom-call | tf_op jit(solution)/shard_map/finish/pallas_call | solution.py:373
  (2 shorter events, 0.0 us)
Async XLA Ops:
  2.4 8.6 %collective-permute-start = (f32[80,256]{1,0:T(8,128)S(1)}, f32[80,256]{1,0:T(8,128)S(1)}, u32[]{:S(2)}, u32[]{:S(2)}) collective-permute-start(f32[80,256]{1,0:T(8,128)S(1)} %get-tuple-element.27), channel_id=1, source_target_pairs={{0,2},{2,4},{4,6},{6,8},{8,10},{10,12},{12,14},{14,16},{16,18},{18... | collective-permute-start | bytes 245768 | tf_op jit(solution)/shard_map/ppermute | solution.py:407
  6.5 4.8 %collective-permute-start.1 = (f32[80,256]{1,0:T(8,128)S(1)}, f32[80,256]{1,0:T(8,128)S(1)}, u32[]{:S(2)}, u32[]{:S(2)}) collective-permute-start(f32[80,256]{1,0:T(8,128)S(1)} %get-tuple-element.28), channel_id=1, source_target_pairs={{2,0},{4,2},{6,4},{8,6},{10,8},{12,10},{14,12},{16,14},{18,16},{20... | collective-permute-start | bytes 245768 | tf_op jit(solution)/shard_map/ppermute | solution.py:422
  11.3 1.5 %collective-permute-start.2 = (f32[80,512]{1,0:T(8,128)S(1)}, f32[80,512]{1,0:T(8,128)S(1)}, u32[]{:S(2)}, u32[]{:S(2)}) collective-permute-start(f32[80,512]{1,0:T(8,128)S(1)} %edges.1.edge_ref), channel_id=1, source_target_pairs={{0,1},{1,0},{2,3},{3,2},{4,5},{5,4},{6,7},{7,6},{8,9},{9,8},{10,11... | collective-permute-start | bytes 491528 | tf_op jit(solution)/shard_map/ppermute | solution.py:451
  14.3 1.4 %collective-permute-start.3 = (f32[152,128]{1,0:T(8,128)S(1)}, f32[152,128]{1,0:T(8,128)S(1)}, u32[]{:S(2)}, u32[]{:S(2)}) collective-permute-start(f32[152,128]{1,0:T(8,128)S(1)} %get-tuple-element.30), channel_id=1, source_target_pairs={{0,1},{1,0},{2,3},{3,2},{4,5},{5,4},{6,7},{7,6},{8,9},{9,8},{10,11... | collective-permute-start | bytes 233480 | tf_op jit(solution)/shard_map/ppermute | solution.py:464

commit v4 on v3

--- a/solution.py
+++ b/solution.py
@@ -287,9 +287,9 @@
         yield
 
 
-def turn_kernel(width, other, side, edge_ref, own_ref, *refs):
+def turn_kernel(width, other, sides, edge_ref, own_ref, *refs):
     half = lax.rem(lax.axis_index("off") + other, 2)
-    for _ in turn(width, half, side, edge_ref, own_ref, refs[-1]):
+    for _ in zip(*[turn(width, half, side, edge_ref, own_ref, refs[-1]) for side in sides]):
         pass
 
 
@@ -434,26 +434,26 @@
     twins = [(i, i ^ 1) for i in range(shares)]
     turned_shape = pltpu.VMEM((LANES // width * WINDOW, 2 * HALF, LANES), bf16)
 
-    def turned(other, side, edge, *before):
+    def turned(other, sides, edge, *before):
         return call(
-            functools.partial(turn_kernel, width, other, side),
-            ("left" if side == 0 else "right") + "_turns",
+            functools.partial(turn_kernel, width, other, sides),
+            "turns",
             turned_shape,
             [vmem] * (2 + len(before)),
             **({"input_output_aliases": {2: 0}} if before else {}),
         )(edge, own, *before)
 
     left = call(functools.partial(edge_kernel, [0]), "edge", half_shape, [vmem, vmem, smem])(own, low, facts[2])
-    window = turned(0, 0, left)
+    window = turned(0, [0], left)
     edges = call(
         functools.partial(edge_kernel, [0, 1]), "edges", pltpu.VMEM((HALF, 4 * LANES), f32), [vmem] * 4
     )(own, low, high, window)
     edges_other = lax.ppermute(edges, "off", twins)
-    window = turned(0, 1, edges, window)
+    window = turned(0, [1], edges, window)
     sum_shape = pltpu.VMEM((points, span), f32)
     tables = [vmem, vmem, smem]
     total = call(functools.partial(first_kernel, 0, classes), "first", sum_shape, tables + [vmem])(*facts, window)
-    window = turned(1, 1, edges_other, turned(1, 0, edges_other))
+    window = turned(1, [0, 1], edges_other)
     shares_out = call(
         second_kernel, "second", [pltpu.VMEM((points, span // shares), f32)] * shares, tables + [vmem] * 2
     )(*facts, window, total)

time: 16.8 us -> 16.7 us (level)
    pallas_call x13 -> x12, Pallas kernels: 11.3 us -> 11.2 us  [call(): run(*map(pltpu.with_memory_space_constraint, operands, places))]
where the time goes in v4:
time: 16.7 us; the launch traced here: 16.5 us
  Pallas kernels  11.2 us (67%)
  starting transfers between devices  4.1 us (25%)
  waiting for transfers between devices  1.07 us (6%)
    pallas_call x12, Pallas kernels, call(): run(*map(pltpu.with_memory_space_constraint, operands, places))  11.2 us
    ppermute x1, starting transfers between devices, local(): high = lax.ppermute(to_left, 'dom', backward)  1.81 us
    ppermute x1, starting transfers between devices, local(): low = lax.ppermute(to_right, 'dom', forward)  1.74 us
    ppermute x1, waiting for transfers between devices, local(): pieces.append(lax.ppermute(shares_out[step], 'off', pairs))  0.92 us
    ppermute x1, starting transfers between devices, local(): pieces.append(lax.ppermute(shares_out[step], 'off', pairs))  0.48 us
  transfers between devices with their start and end apart: 4, of which 2 were waited for; matrix products, arithmetic and copies ran while one was open for 0% of the time, Pallas kernels for 39%

profile of v4, /device:TPU:0, one launch (start us, length us, event | category | flops | bytes accessed | tf_op | source)
XLA Modules:
  0.0 16.5 jit_solution(16984434249683744581)
XLA Ops:
  0.0 1.1 %table.1 = (f32[80,256]{1,0:T(8,128)S(1)}, f32[80,256]{1,0:T(8,128)S(1)}) custom-call(s32[24]{0:T(128)} %slot_hbm.7, f32[24,2432]{1,0:T(8,128)} %contrib_hbm.7), custom_call_target="tpu_custom_call" | custom-call | tf_op jit(solution)/shard_map/table/pallas_call | solution.py:373
  1.1 1.3 %own.1 = (f32[2,80,384]{2,1,0:T(8,128)S(1)}, f32[80,256]{1,0:T(8,128)S(1)}) custom-call(s32[24]{0:T(128)} %slot_hbm.7, f32[24,2432]{1,0:T(8,128)} %contrib_hbm.7, f32[80,256]{1,0:T(8,128)S(1)} %get-tuple-element.18._sent), custom_call_target="tpu_custom_call", output_to_operand_aliasing={{1}: (2, {})} | custom-call | tf_op jit(solution)/shard_map/own/pallas_call | solution.py:373
  2.4 1.7 %collective-permute-start = (f32[80,256]{1,0:T(8,128)S(1)}, f32[80,256]{1,0:T(8,128)S(1)}, u32[]{:S(2)}, u32[]{:S(2)}) collective-permute-start(f32[80,256]{1,0:T(8,128)S(1)} %get-tuple-element.27), channel_id=1, source_target_pairs={{0,2},{2,4},{4,6},{6,8},{8,10},{10,12},{12,14},{14,16},{16,18},{18... | collective-permute-start | bytes 245768 | tf_op jit(solution)/shard_map/ppermute | solution.py:407
  4.1 2.3 %early.1 = (bf16[40,2,152,256]{3,2,1,0:T(8,128)(2,1)S(1)}, f32[2,80,384]{2,1,0:T(8,128)S(1)}, f32[80,256]{1,0:T(8,128)S(1)}) custom-call(s32[24]{0:T(128)} %slot_hbm.7, f32[24,2432]{1,0:T(8,128)} %contrib_hbm.7, f32[40,152,152]{2,1,0:T(8,128)} %block_hbm.3, f32[2,80,384]{2,1,0:T(8,128)S(1)} %get-tuple-element.19._own, ...), custom_call_target="tpu_custom_call", output_to_operand_aliasing={{1}: (3, {}), {2}: (4, {})} | custom-call | tf_op jit(solution)/shard_map/early/pallas_call | solution.py:373
  6.5 1.8 %collective-permute-start.1 = (f32[80,256]{1,0:T(8,128)S(1)}, f32[80,256]{1,0:T(8,128)S(1)}, u32[]{:S(2)}, u32[]{:S(2)}) collective-permute-start(f32[80,256]{1,0:T(8,128)S(1)} %get-tuple-element.28), channel_id=1, source_target_pairs={{2,0},{4,2},{6,4},{8,6},{10,8},{12,10},{14,12},{16,14},{18,16},{20... | collective-permute-start | bytes 245768 | tf_op jit(solution)/shard_map/ppermute | solution.py:422
  8.3 2.6 %late.1 = (bf16[40,2,152,256]{3,2,1,0:T(8,128)(2,1)S(1)}, f32[2,80,384]{2,1,0:T(8,128)S(1)}, f32[40,256]{1,0:T(8,128)S(1)}, s32[40]{0:T(128)S(4)}) custom-call(s32[16,40]{1,0:T(8,128)} %src_hbm.1, s32[16,40]{1,0:T(8,128)} %class_hbm.1, s32[24]{0:T(128)} %slot_hbm.7, f32[24,2432]{1,0:T(8,128)} %contrib_hbm.7, ...), custom_call_target="tpu_custom_call", output_to_operand_aliasing={{0}: (5, {}), {1}: (6, {})} | custom-call | tf_op jit(solution)/shard_map/late/pallas_call | solution.py:373
  10.9 0.0 collective-permute-done.refs_0_
  10.9 0.3 %turns.3.refs_2_.refs_0_ = bf16[40,160,128]{2,1,0:T(8,128)(2,1)S(1)} custom-call(f32[80,256]{1,0:T(8,128)S(1)} %edge.1.edge_ref, f32[2,80,384]{2,1,0:T(8,128)S(1)} %get-tuple-element.26.own_ref), custom_call_target="tpu_custom_call" | custom-call | tf_op jit(solution)/shard_map/turns/pallas_call | solution.py:373
  11.2 0.0 collective-permute-done.1.refs_1_
  11.3 0.1 collective-permute-start.2
  11.4 0.2 %turns.5.shifted = bf16[40,160,128]{2,1,0:T(8,128)(2,1)S(1)} custom-call(f32[80,512]{1,0:T(8,128)S(1)} %edges.1.edge_ref, f32[2,80,384]{2,1,0:T(8,128)S(1)} %get-tuple-element.26.own_ref, bf16[40,160,128]{2,1,0:T(8,128)(2,1)S(1)} %turns.3.refs_2_.refs_0_), custom_call_target="tpu_custom_call", output_to_operand_aliasing={{}: (2, {})} | custom-call | tf_op jit(solution)/shard_map/turns/pallas_call | solution.py:373
  11.6 1.0 %first.1.before = f32[152,256]{1,0:T(8,128)S(1)} custom-call(bf16[40,2,152,256]{3,2,1,0:T(8,128)(2,1)S(1)} %get-tuple-element.23.split_ref, f32[40,256]{1,0:T(8,128)S(1)} %get-tuple-element.24.mask_ref, s32[40]{0:T(128)S(4)} %get-tuple-element.25.refs_1_.place_ref, bf16[40,160,128]{2,1,0:T(8,128)(2,1)S(1)} %turns.5.shifted), custom_call_target="tpu_custom_call" | custom-call | tf_op jit(solution)/shard_map/first/pallas_call | solution.py:373
  12.6 0.1 collective-permute-done.2.edge_ref
  12.7 0.5 %turns.4.shifted = bf16[40,160,128]{2,1,0:T(8,128)(2,1)S(1)} custom-call(f32[80,512]{1,0:T(8,128)S(1)} %collective-permute-done.2.edge_ref, f32[2,80,384]{2,1,0:T(8,128)S(1)} %get-tuple-element.26.own_ref), custom_call_target="tpu_custom_call" | custom-call | tf_op jit(solution)/shard_map/turns/pallas_call | solution.py:373
  13.2 1.1 %second.1 = (f32[152,128]{1,0:T(8,128)S(1)}, f32[152,128]{1,0:T(8,128)S(1)}) custom-call(bf16[40,2,152,256]{3,2,1,0:T(8,128)(2,1)S(1)} %get-tuple-element.23.split_ref, f32[40,256]{1,0:T(8,128)S(1)} %get-tuple-element.24.mask_ref, s32[40]{0:T(128)S(4)} %get-tuple-element.25.refs_1_.place_ref, bf16[40,160,128]{2,1,0:T(8,128)(2,1)S(1)} %turns.4.shifted, ...), custom_call_target="tpu_custom_call" | custom-call | tf_op jit(solution)/shard_map/second/pallas_call | solution.py:373
  14.3 0.5 %collective-permute-start.3 = (f32[152,128]{1,0:T(8,128)S(1)}, f32[152,128]{1,0:T(8,128)S(1)}, u32[]{:S(2)}, u32[]{:S(2)}) collective-permute-start(f32[152,128]{1,0:T(8,128)S(1)} %get-tuple-element.30), channel_id=1, source_target_pairs={{0,1},{1,0},{2,3},{3,2},{4,5},{5,4},{6,7},{7,6},{8,9},{9,8},{10,11... | collective-permute-start | bytes 233480 | tf_op jit(solution)/shard_map/ppermute | solution.py:464
  14.8 0.9 %collective-permute-done.3.refs_1_ = f32[152,128]{1,0:T(8,128)S(1)} collective-permute-done((f32[152,128]{1,0:T(8,128)S(1)}, f32[152,128]{1,0:T(8,128)S(1)}, u32[]{:S(2)}, u32[]{:S(2)}) %collective-permute-start.3) | collective-permute-done | bytes 77856 | tf_op jit(solution)/shard_map/ppermute | solution.py:464
  15.7 0.8 %finish.1 = f32[8,2432]{1,0:T(8,128)} custom-call(f32[152,128]{1,0:T(8,128)S(1)} %get-tuple-element.29.refs_0_, f32[152,128]{1,0:T(8,128)S(1)} %collective-permute-done.3.refs_1_), custom_call_target="tpu_custom_call" | custom-call | tf_op jit(solution)/shard_map/finish/pallas_call | solution.py:373
  (2 shorter events, 0.0 us)
Async XLA Ops:
  2.4 8.6 %collective-permute-start = (f32[80,256]{1,0:T(8,128)S(1)}, f32[80,256]{1,0:T(8,128)S(1)}, u32[]{:S(2)}, u32[]{:S(2)}) collective-permute-start(f32[80,256]{1,0:T(8,128)S(1)} %get-tuple-element.27), channel_id=1, source_target_pairs={{0,2},{2,4},{4,6},{6,8},{8,10},{10,12},{12,14},{14,16},{16,18},{18... | collective-permute-start | bytes 245768 | tf_op jit(solution)/shard_map/ppermute | solution.py:407
  6.5 4.8 %collective-permute-start.1 = (f32[80,256]{1,0:T(8,128)S(1)}, f32[80,256]{1,0:T(8,128)S(1)}, u32[]{:S(2)}, u32[]{:S(2)}) collective-permute-start(f32[80,256]{1,0:T(8,128)S(1)} %get-tuple-element.28), channel_id=1, source_target_pairs={{2,0},{4,2},{6,4},{8,6},{10,8},{12,10},{14,12},{16,14},{18,16},{20... | collective-permute-start | bytes 245768 | tf_op jit(solution)/shard_map/ppermute | solution.py:422
  11.3 1.5 %collective-permute-start.2 = (f32[80,512]{1,0:T(8,128)S(1)}, f32[80,512]{1,0:T(8,128)S(1)}, u32[]{:S(2)}, u32[]{:S(2)}) collective-permute-start(f32[80,512]{1,0:T(8,128)S(1)} %edges.1.edge_ref), channel_id=1, source_target_pairs={{0,1},{1,0},{2,3},{3,2},{4,5},{5,4},{6,7},{7,6},{8,9},{9,8},{10,11... | collective-permute-start | bytes 491528 | tf_op jit(solution)/shard_map/ppermute | solution.py:451
  14.3 1.4 %collective-permute-start.3 = (f32[152,128]{1,0:T(8,128)S(1)}, f32[152,128]{1,0:T(8,128)S(1)}, u32[]{:S(2)}, u32[]{:S(2)}) collective-permute-start(f32[152,128]{1,0:T(8,128)S(1)} %get-tuple-element.30), channel_id=1, source_target_pairs={{0,1},{1,0},{2,3},{3,2},{4,5},{5,4},{6,7},{7,6},{8,9},{9,8},{10,11... | collective-permute-start | bytes 233480 | tf_op jit(solution)/shard_map/ppermute | solution.py:464
